TPU v7x, 32 devices: a whole 2x2x4 slice. The times are simulated.
32 devices in a mesh: blk: 8 (over z, x), tok: 4 (over y, core).
Axes of the slice: x: 2, y: 2, z: 4, core: 2. Of those that a mesh axis runs over, the one named last changes fastest.
Arguments:
- acts: bfloat16 [1024, 2, 14336], P('tok', None, 'blk'), may hold values from -6 to 6
Outputs:
- hessian: bfloat16 [2, 14336, 28672], P(None, ('blk', 'tok'))
All inputs are finite; a program needn't handle non-finite values.
Results may differ from a plain program's by a relative error of at most 0.0085.
Values may be sent and summed in bfloat16 or wider, within the bound.
No kernel may reach another device: no remote copies, remote signals or barrier semaphores. Data moves between devices by JAX's collectives and lax.ppermute only.
A program may use at most 384 MiB of HBM per device.

v0:
```python
import functools

import jax
import jax.numpy as jnp
from jax import lax
from jax.experimental import pallas as pl
from jax.experimental.pallas import tpu as pltpu
from jax.sharding import PartitionSpec as P

LANES = 128
KSCALE = 1
CALLS = (2, 3, 5, 6, 7, 8, 9, 10)
VMEM = 56 * 2**20


def picked(ref, at):
    return ref if at is None else ref.at[at]


def left_kernel(count, picks, tok_ref, *refs):
    parts, out_ref, held, sems = refs[: 2 * count], refs[-3], refs[-2], refs[-1]
    strip = out_ref.shape[1]
    window = held.shape[2]
    first = tok_ref[0] * strip
    base = pl.multiple_of(first // LANES * LANES, LANES)
    copies = []
    for h in range(2):
        at = 0
        for i, ref in enumerate(parts[h * count : (h + 1) * count]):
            depth = ref.shape[-2]
            copies.append(
                pltpu.make_async_copy(
                    picked(ref, picks[h * count + i]).at[:, pl.ds(base, window)], held.at[h, at : at + depth], sems.at[h, i]
                )
            )
            at += depth
    for copy in copies:
        copy.start()
    row = lax.broadcasted_iota(jnp.int32, (strip, window), 0)
    col = lax.broadcasted_iota(jnp.int32, (strip, window), 1)
    pick = jnp.where(col == row + (first - base), 1.0, 0.0).astype(jnp.bfloat16)
    for copy in copies:
        copy.wait()
    for h in range(2):
        part = lax.dot_general(
            pick, held[h], (((1,), (1,)), ((), ())), preferred_element_type=jnp.float32
        )
        out_ref[h] = part.astype(out_ref.dtype)


def left_rows(tok, parts, strip):
    picks = [p[1] for p in parts]
    parts = [p[0] for p in parts]
    depth = sum(p.shape[-2] for p in parts) // 2
    shape = (2, strip, depth)
    window = (strip + LANES // 2 + LANES - 1) // LANES * LANES
    return pl.pallas_call(
        functools.partial(left_kernel, len(parts) // 2, picks),
        out_shape=jax.ShapeDtypeStruct(shape, jnp.bfloat16),
        in_specs=[pl.BlockSpec(memory_space=pltpu.SMEM)]
        + [pl.BlockSpec(memory_space=pl.ANY)] * len(parts),
        out_specs=pl.BlockSpec(memory_space=pltpu.VMEM),
        scratch_shapes=[
            pltpu.VMEM((2, depth, window), jnp.bfloat16),
            pltpu.SemaphoreType.DMA((2, len(parts) // 2)),
        ],
        compiler_params=pltpu.CompilerParams(vmem_limit_bytes=VMEM),
        cost_estimate=pl.CostEstimate(
            flops=2 * 2 * strip * depth * window,
            bytes_accessed=2 * 2 * depth * (window + strip),
            transcendentals=0,
        ),
    )(tok[None], *parts)


def column_kernel(factor, parts, picks, cols_ref, left_ref, *refs):
    blocks = len(parts)
    count = sum(len(p) for p in parts)
    rights, out_ref, held, sems = refs[:count], refs[-3], refs[-2], refs[-1]
    block, half = pl.program_id(0), pl.program_id(1)
    last = pl.num_programs(1) - 1

    def copies(b):
        first = sum(len(p) for p in parts[:b])
        at, found = 0, []
        for i, depth in enumerate(parts[b]):
            found.append(
                pltpu.make_async_copy(
                    picked(rights[first + i], picks[b][i]),
                    held.at[b % 2, at : at + depth],
                    sems.at[b % 2, i],
                )
            )
            at += depth
        return found

    @pl.when((block == 0) & (half == 0))
    def _():
        for b in range(min(2, blocks)):
            for copy in copies(b):
                copy.start()

    for b in range(blocks):

        @pl.when((block == b) & (half == 0))
        def _(b=b):
            for copy in copies(b):
                copy.wait()

    part = jnp.dot(left_ref[...], held[block % 2], preferred_element_type=jnp.float32)
    out_ref[...] = (part * factor).astype(out_ref.dtype)
    for b in range(blocks - 2):

        @pl.when((block == b) & (half == last))
        def _(b=b):
            for copy in copies(b + 2):
                copy.start()


def column_blocks(out, left, groups, cols, width, factor):
    block = groups[0][0][0].shape[-1]
    halves, strip, depth = left.shape
    parts = [[a.shape[-2] for a, _ in g] for g in groups]
    picks = [[at for _, at in g] for g in groups]
    anywhere = pl.BlockSpec(memory_space=pl.ANY)
    operands = [cols, left] + [a for g in groups for a, _ in g]
    in_specs = [pl.BlockSpec((None, strip, depth), lambda b, i, c: (i, 0, 0))]
    in_specs += [anywhere] * (len(operands) - 2)
    aliases = {}
    if out is not None:
        in_specs.append(anywhere)
        aliases = {len(operands): 0}
        operands.append(out)
    return pl.pallas_call(
        functools.partial(column_kernel, factor, parts, picks),
        out_shape=jax.ShapeDtypeStruct((2, strip, width), jnp.bfloat16),
        grid_spec=pltpu.PrefetchScalarGridSpec(
            num_scalar_prefetch=1,
            grid=(len(groups), halves),
            in_specs=in_specs,
            out_specs=pl.BlockSpec((None, strip, block), lambda b, i, c: (i, 0, c[b])),
            scratch_shapes=[
                pltpu.VMEM((min(2, len(groups)), depth, block), jnp.bfloat16),
                pltpu.SemaphoreType.DMA((2, max(len(p) for p in parts))),
            ],
        ),
        input_output_aliases=aliases,
        compiler_params=pltpu.CompilerParams(vmem_limit_bytes=VMEM),
        cost_estimate=pl.CostEstimate(
            flops=int(KSCALE * 2 * 2 * strip * depth * block * len(groups)),
            bytes_accessed=2 * (depth * (block + 2 * strip) + 2 * strip * block) * len(groups),
            transcendentals=0,
        ),
    )(*operands)


def gathered(acts):
    nblk, ntok = lax.axis_size("blk"), lax.axis_size("tok")
    tok_rows, _, rows = acts.shape
    strip = rows // ntok
    tok = lax.axis_index("tok")
    halves = jnp.swapaxes(acts, 0, 1)
    group = lax.all_gather(halves, "tok", axis=0)
    left = lax.dynamic_slice_in_dim(group, tok * strip, strip, 3)
    whole = lax.all_gather(group, "blk", axis=0)
    order = jnp.concatenate([whole[:, :, 0], whole[::-1, :, 1]], axis=0)
    product = jnp.einsum("thks,ctkr->hscr", left, order, preferred_element_type=jnp.float32)
    scaled = (product * (2.0 / (tok_rows * ntok))).astype(jnp.bfloat16)
    return scaled.reshape(2, strip, 2 * nblk * rows)


STEPS = [
    (("S", 1, 0), ("X", 0, 1), ("Y", 0, 0)),
    (("S", 1, 1), ("X", 0, 0), ("Y", 0, 1)),
    (("S", 2, 0), ("D", 0, 0), ("D", 0, 1)),
    (("S", 2, 1), ("X", 1, 0), ("Y", 1, 0)),
    (("S", 3, 0), ("X", 1, 1), ("Y", 1, 1)),
    (("S", 3, 1), ("X", 2, 0), ("Y", 2, 0)),
    (("D", 1, 0), ("X", 2, 1), ("Y", 2, 1)),
    (("D", 1, 1), ("X", 3, 1), ("Y", 3, 0)),
    (("D", 2, 0), ("X", 3, 0), ("Y", 3, 1)),
    (("D", 2, 1), ("D", 3, 0), ("D", 3, 1)),
]


def source(link, name):
    place, k, h = name
    if link == 0:
        return place, k - 1, h
    if place == "D":
        return ("Y" if link == 1 else "X"), k, h
    return "S", k, h


def meshed(acts):
    nblk, ntok = lax.axis_size("blk"), lax.axis_size("tok")
    nz = nblk // 2
    tok_rows, _, rows = acts.shape
    strip = rows // ntok
    width = 2 * nblk * rows
    factor = 2.0 / (tok_rows * ntok)
    axes = ("blk", "tok")
    places = [
        (z, x, y, c)
        for z in range(nz)
        for x in range(2)
        for y in range(2)
        for c in range(2)
    ]

    def at(z, x, y, c):
        return ((z * 2 + x) * 2 + y) * 2 + c

    links = [
        [(at(z, x, y, c), at((z + 1) % nz, x, y, c)) for z, x, y, c in places],
        [(at(z, x, y, c), at(z, 1 - x, y, c)) for z, x, y, c in places],
        [(at(z, x, y, c), at(z, x, 1 - y, c)) for z, x, y, c in places],
    ]
    cores = [(at(z, x, y, c), at(z, x, y, 1 - c)) for z, x, y, c in places]

    blk, tok = lax.axis_index("blk"), lax.axis_index("tok")
    z, x = blk // 2, blk % 2
    cols = []
    for k in range(nz):
        zk = (z - k) % nz
        for xk in (x, 1 - x):
            cols += [2 * zk + xk, 2 * nblk - 1 - (2 * zk + xk)]
    cols = [c.astype(jnp.int32) for c in cols]

    own = lax.optimization_barrier((acts[:, 0, :], acts[:, 1, :]))
    mine = {("S", 0, 0): own[0], ("S", 0, 1): own[1]}
    other = {}
    ready = {("S", 0, 0): 0, ("S", 0, 1): 0}

    out, left = None, None
    pending = {}
    for i, step in enumerate(STEPS):
        for name in step:
            ready[name] = i + 1
    todo = []
    for k in range(nz):
        for xi, (near, far) in enumerate((("S", "Y"), ("X", "D"))):
            for h in range(2):
                todo.append((max(ready[near, k, h], ready[far, k, h]), (near, k, h), (far, k, h), (2 * k + xi) * 2 + h))
    todo.sort()
    calls, first = [], 0
    for upto in CALLS:
        end = sum(t[0] <= upto for t in todo)
        ends = [first + 1, end] if upto + 1 == len(STEPS) else [end]
        for stop in ends:
            calls.append([t[3] for t in todo[first:stop]])
            first = stop
    cols = [jnp.stack([cols[w] for w in call]) for call in calls]

    def start(i):
        for link, name in enumerate(STEPS[i]):
            pending[name] = lax.ppermute(mine[source(link, name)], axes, links[link])

    def parts_of(near, far):
        return [(mine[near], None), other[near], (mine[far], None), other[far]]

    def due(upto):
        now = [t for t in todo if t[0] <= upto]
        del todo[: len(now)]
        return [parts_of(near, far) for _, near, far, _ in now]

    def swap(given, groups, out):
        arrays = [[a for a, _ in g] for g in groups]
        picks = [[at for _, at in g] for g in groups]

        def run(given, arrays, out, column, left):
            given = lax.ppermute(jnp.stack(given), axes, cores)
            if picks:
                pairs = [list(zip(a, p)) for a, p in zip(arrays, picks)]
                out = column_blocks(out, left, pairs, column, width, factor)
            return given, out

        def skip(given, arrays, out, column, left):
            return jnp.stack(given), out

        column = cols.pop(0) if groups else None
        return lax.cond(cols[-1][0] >= 0, run, skip, given, arrays, out, column, left)

    start(0)
    swapped, _ = swap(list(own), [], None)
    start(1)
    for i, step in enumerate(STEPS):
        final = i + 1 == len(STEPS)
        if final:
            groups = due(i)
            out = column_blocks(out, left, groups[:1], cols.pop(0), width, factor)
            cols, out = lax.optimization_barrier((cols, out))
        arrived = [pending.pop(name) for name in step]
        if i == 0:
            swapped, arrived, cols = lax.optimization_barrier((swapped, arrived, cols))
            other.update((("S", 0, h), (swapped, h)) for h in range(2))
        else:
            arrived, cols = lax.optimization_barrier((arrived, cols))
        mine.update(zip(step, arrived))
        if final:
            for name, a in zip(step, arrived):
                other[name] = (lax.ppermute(a, axes, cores), None)
            out = column_blocks(out, left, groups[1:], cols.pop(0), width, factor)
            break
        inside = i in CALLS and out is not None
        swapped, new = swap(arrived, due(i) if inside else [], out if inside else None)
        if inside:
            out = new
        other.update((name, (swapped, j)) for j, name in enumerate(step))
        if i in CALLS and not inside:
            if left is None:
                parts = [p for h in range(2) for p in parts_of(("S", 0, h), ("Y", 0, h))]
                left = left_rows(tok, parts, strip)
            out = column_blocks(out, left, due(i), cols.pop(0), width, factor)
        names = []
        if i + 2 < len(STEPS):
            names = sorted({source(link, name) for link, name in enumerate(STEPS[i + 2])})
        held = ([mine[n] for n in names], swapped, cols, out)
        held, swapped, cols, out = lax.optimization_barrier(held)
        mine.update(zip(names, held))
        other.update((name, (swapped, j)) for j, name in enumerate(step))
        if i + 2 < len(STEPS):
            start(i + 2)
    return column_blocks(out, left, due(len(STEPS)), cols.pop(0), width, factor)


def local(acts):
    if lax.axis_size("blk") == 8 and lax.axis_size("tok") == 4 and acts.shape[2] == 14 * LANES:
        return meshed(acts)
    return gathered(acts)


def solution(mesh):
    return jax.shard_map(
        local,
        mesh=mesh,
        in_specs=(P("tok", None, "blk"),),
        out_specs=P(None, ("blk", "tok"), None),
        check_vma=False,
    )
```

profile of v0, /device:TPU:0, one launch (start us, length us, event | category | flops | bytes accessed | tf_op | source)
XLA Modules:
  0.0 248.0 jit_solution(6331284938591595817)
XLA Ops:
  13.0 5.4 %conditional.10 = (bf16[2,256,1792]{2,1,0:T(8,128)(2,1)}) conditional(s32[]{:T(128)} %convert_element_type.57, (bf16[256,1792]{1,0:T(8,128)(2,1)}, bf16[256,1792]{1,0:T(8,128)(2,1)S(1)}) %tuple.94, (bf16[256,1792]{1,0:T(8,128)(2,1)}, bf16[256,1792]{1,0:T(8,128)(2,1)S(1)}) %tuple.94), branch_computations={%region_0.1_spmd, %region_1.2_spmd} | conditional | flops 917504 | bytes 11010096 | solution.py:282
  20.2 10.7 %collective-permute-done.12.refs_2_ = bf16[256,1792]{1,0:T(8,128)(2,1)} collective-permute-done((bf16[256,1792]{1,0:T(8,128)(2,1)}, bf16[256,1792]{1,0:T(8,128)(2,1)}, u32[]{:S(2)}, u32[]{:S(2)}) %collective-permute-start.12) | collective-permute-done | bytes 917536 | tf_op jit(solution)/shard_map/ppermute | solution.py:257
  34.4 7.3 %conditional.11 = (bf16[3,256,1792]{2,1,0:T(8,128)(2,1)}) conditional(s32[]{:T(128)} %bitcast.76, (bf16[256,1792]{1,0:T(8,128)(2,1)}, bf16[256,1792]{1,0:T(8,128)(2,1)}, bf16[256,1792]{1,0:T(8,128)(2,1)}) %tuple.96, (bf16[256,1792]{1,0:T(8,128)(2,1)}, bf16[256,1792]{1,0:T(8,128)(2,1)}, bf16[256,1792]{1,0:T(8,128)(2,1)}) %tuple.96), branch_computations={%region_2.3_spmd, %region_3.4_spmd} | conditional | flops 2752512 | bytes 16515120 | solution.py:282
  36.5 5.2 %collective-permute-done.1 = bf16[3,256,1792]{2,1,0:T(8,128)(2,1)} collective-permute-done((bf16[3,256,1792]{2,1,0:T(8,128)(2,1)S(1)}, bf16[3,256,1792]{2,1,0:T(8,128)(2,1)}, u32[]{:S(2)}, u32[]{:S(2)}) %collective-permute-start.1) | collective-permute-done | bytes 2752544 | tf_op jit(solution)/shard_map/cond/branch_1_fun/ppermute | solution.py:272
  43.8 8.4 %collective-permute-done.17 = bf16[256,1792]{1,0:T(8,128)(2,1)} collective-permute-done((bf16[256,1792]{1,0:T(8,128)(2,1)}, bf16[256,1792]{1,0:T(8,128)(2,1)}, u32[]{:S(2)}, u32[]{:S(2)}) %collective-permute-start.17) | collective-permute-done | bytes 917536 | tf_op jit(solution)/shard_map/ppermute | solution.py:257
  56.4 7.3 %conditional.12 = (bf16[3,256,1792]{2,1,0:T(8,128)(2,1)}) conditional(s32[]{:T(128)} %bitcast.77, (bf16[256,1792]{1,0:T(8,128)(2,1)}, bf16[256,1792]{1,0:T(8,128)(2,1)}, bf16[256,1792]{1,0:T(8,128)(2,1)}) %tuple.99, (bf16[256,1792]{1,0:T(8,128)(2,1)}, bf16[256,1792]{1,0:T(8,128)(2,1)}, bf16[256,1792]{1,0:T(8,128)(2,1)}) %tuple.99), branch_computations={%region_4.5_spmd, %region_5.6_spmd} | conditional | flops 2752512 | bytes 16515120 | solution.py:282
  75.9 7.3 %conditional.13 = (bf16[3,256,1792]{2,1,0:T(8,128)(2,1)}) conditional(s32[]{:T(128)} %bitcast.78, (bf16[256,1792]{1,0:T(8,128)(2,1)}, bf16[256,1792]{1,0:T(8,128)(2,1)}, bf16[256,1792]{1,0:T(8,128)(2,1)}) %tuple.102, (bf16[256,1792]{1,0:T(8,128)(2,1)}, bf16[256,1792]{1,0:T(8,128)(2,1)}, bf16[256,1792]{1,0:T(8,128)(2,1)}) %tuple.102), branch_computations={%region_6.7_spmd, %region_7.8_spmd} | conditional | flops 2752512 | bytes 16515120 | solution.py:282
  83.2 11.4 %shard_map.18 = bf16[2,448,28672]{2,1,0:T(8,128)(2,1)} custom-call(s32[2]{0:T(128)} %get-tuple-element.612.cols_ref, bf16[2,448,1024]{2,1,0:T(8,128)(2,1)S(1)} %shard_map.17.left_ref, bf16[256,1792]{1,0:T(8,128)(2,1)} %get-tuple-element.553.refs_0_, bf16[2,256,1792]{2,1,0:T(8,128)(2,1)} %get-tuple-element.787.refs_1_.refs_5_, ...), custom_call_target="tpu_custom_call" | custom-call | flops 6576668672 | bytes 17432576 | tf_op jit(solution)/shard_map/pallas_call | solution.py:134
  98.3 13.6 %conditional.14 = (bf16[3,256,1792]{2,1,0:T(8,128)(2,1)}, bf16[2,448,28672]{2,1,0:T(8,128)(2,1)}) conditional(s32[]{:T(128)} %bitcast.80, (bf16[256,1792]{1,0:T(8,128)(2,1)}, bf16[256,1792]{1,0:T(8,128)(2,1)}, bf16[256,1792]{1,0:T(8,128)(2,1)}, bf16[2,448,28672]{2,1,0:T(8,128)(2,1)}) %tuple.105, (bf16[256,1792]{1,0:T(8,128)(2,1)}, ...), branch_computations={%region_8.9_spmd, %region_9.10_spmd} | conditional | flops 6579421184 | bytes 33947704 | solution.py:282
  100.6 11.3 %branch_1_fun.5 = bf16[2,448,28672]{2,1,0:T(8,128)(2,1)} custom-call(s32[2]{0:T(128)S(1)} %get-tuple-element.267.cols_ref, bf16[2,448,1024]{2,1,0:T(8,128)(2,1)S(1)} %get-tuple-element.268.left_ref, bf16[256,1792]{1,0:T(8,128)(2,1)} %get-tuple-element.269.refs_0_, bf16[3,256,1792]{2,1,0:T(8,128)(2,1)} %get-tuple-element.270.refs_1_, ...), custom_call_target="tpu_custom_call", output_to_operand_aliasing={{}: (10, {})} | custom-call | flops 6576668672 | bytes 17432576 | tf_op jit(solution)/shard_map/cond/branch_1_fun/pallas_call | solution.py:134
  121.4 7.1 %conditional.15 = (bf16[3,256,1792]{2,1,0:T(8,128)(2,1)}) conditional(s32[]{:T(128)} %bitcast.81, (bf16[256,1792]{1,0:T(8,128)(2,1)S(1)}, bf16[256,1792]{1,0:T(8,128)(2,1)}, bf16[256,1792]{1,0:T(8,128)(2,1)}) %tuple.109, (bf16[256,1792]{1,0:T(8,128)(2,1)S(1)}, bf16[256,1792]{1,0:T(8,128)(2,1)}, bf16[256,1792]{1,0:T(8,128)(2,1)}) %tuple.109), branch_computations={%region_10.11_spmd, %region_11.12_spmd} | conditional | flops 2752512 | bytes 16515120 | solution.py:282
  129.4 10.3 %collective-permute-done.25.refs_0_ = bf16[256,1792]{1,0:T(8,128)(2,1)} collective-permute-done((bf16[256,1792]{1,0:T(8,128)(2,1)}, bf16[256,1792]{1,0:T(8,128)(2,1)}, u32[]{:S(2)}, u32[]{:S(2)}) %collective-permute-start.25) | collective-permute-done | bytes 917536 | tf_op jit(solution)/shard_map/ppermute | solution.py:257
  141.2 13.4 %conditional.16 = (bf16[3,256,1792]{2,1,0:T(8,128)(2,1)}, bf16[2,448,28672]{2,1,0:T(8,128)(2,1)}) conditional(s32[]{:T(128)} %bitcast.82, (bf16[256,1792]{1,0:T(8,128)(2,1)}, bf16[256,1792]{1,0:T(8,128)(2,1)}, bf16[256,1792]{1,0:T(8,128)(2,1)}, bf16[2,448,28672]{2,1,0:T(8,128)(2,1)}) %tuple.112, (bf16[256,1792]{1,0:T(8,128)(2,1)}, ...), branch_computations={%region_12.13_spmd, %region_13.14_spmd} | conditional | flops 6579421184 | bytes 33947704 | solution.py:282
  143.3 11.3 %branch_1_fun.6 = bf16[2,448,28672]{2,1,0:T(8,128)(2,1)} custom-call(s32[2]{0:T(128)S(1)} %get-tuple-element.290.cols_ref, bf16[2,448,1024]{2,1,0:T(8,128)(2,1)S(1)} %get-tuple-element.291.left_ref, bf16[256,1792]{1,0:T(8,128)(2,1)} %get-tuple-element.292.refs_0_, bf16[3,256,1792]{2,1,0:T(8,128)(2,1)} %get-tuple-element.293.refs_1_, ...), custom_call_target="tpu_custom_call", output_to_operand_aliasing={{}: (10, {})} | custom-call | flops 6576668672 | bytes 17432576 | tf_op jit(solution)/shard_map/cond/branch_1_fun/pallas_call | solution.py:134
  163.3 9.1 %conditional.17 = (bf16[3,256,1792]{2,1,0:T(8,128)(2,1)}, bf16[2,448,28672]{2,1,0:T(8,128)(2,1)}) conditional(s32[]{:T(128)} %bitcast.83, (bf16[256,1792]{1,0:T(8,128)(2,1)}, bf16[256,1792]{1,0:T(8,128)(2,1)}, bf16[256,1792]{1,0:T(8,128)(2,1)}, bf16[2,448,28672]{2,1,0:T(8,128)(2,1)}) %tuple.116, (bf16[256,1792]{1,0:T(8,128)(2,1)}, ...), branch_computations={%region_14.15_spmd, %region_15.16_spmd} | conditional | flops 3291086848 | bytes 25231416 | solution.py:282
  165.4 7.0 %branch_1_fun.7 = bf16[2,448,28672]{2,1,0:T(8,128)(2,1)} custom-call(s32[1]{0:T(128)} %get-tuple-element.308.cols_ref, bf16[2,448,1024]{2,1,0:T(8,128)(2,1)S(1)} %get-tuple-element.309.left_ref, bf16[256,1792]{1,0:T(8,128)(2,1)} %get-tuple-element.310.refs_0_, bf16[3,256,1792]{2,1,0:T(8,128)(2,1)} %get-tuple-element.311.refs_1_, ...), custom_call_target="tpu_custom_call", output_to_operand_aliasing={{}: (6, {})} | custom-call | flops 3288334336 | bytes 8716288 | tf_op jit(solution)/shard_map/cond/branch_1_fun/pallas_call | solution.py:134
  174.0 5.9 %collective-permute-done.28 = bf16[256,1792]{1,0:T(8,128)(2,1)} collective-permute-done((bf16[256,1792]{1,0:T(8,128)(2,1)}, bf16[256,1792]{1,0:T(8,128)(2,1)}, u32[]{:S(2)}, u32[]{:S(2)}) %collective-permute-start.28) | collective-permute-done | bytes 917536 | tf_op jit(solution)/shard_map/ppermute | solution.py:257
  183.0 13.4 %conditional.18 = (bf16[3,256,1792]{2,1,0:T(8,128)(2,1)}, bf16[2,448,28672]{2,1,0:T(8,128)(2,1)}) conditional(s32[]{:T(128)} %bitcast.84, (bf16[256,1792]{1,0:T(8,128)(2,1)}, bf16[256,1792]{1,0:T(8,128)(2,1)}, bf16[256,1792]{1,0:T(8,128)(2,1)}, bf16[2,448,28672]{2,1,0:T(8,128)(2,1)}) %tuple.120, (bf16[256,1792]{1,0:T(8,128)(2,1)}, ...), branch_computations={%region_16.17_spmd, %region_17.18_spmd} | conditional | flops 6579421184 | bytes 33947704 | solution.py:282
  185.1 11.3 %branch_1_fun.8 = bf16[2,448,28672]{2,1,0:T(8,128)(2,1)} custom-call(s32[2]{0:T(128)S(1)} %get-tuple-element.322.cols_ref, bf16[2,448,1024]{2,1,0:T(8,128)(2,1)S(1)} %get-tuple-element.323.left_ref, bf16[256,1792]{1,0:T(8,128)(2,1)} %get-tuple-element.324.refs_0_, ...), custom_call_target="tpu_custom_call", output_to_operand_aliasing={{}: (10, {})} | custom-call | flops 6576668672 | bytes 17432576 | tf_op jit(solution)/shard_map/cond/branch_1_fun/pallas_call | solution.py:134
  201.9 13.6 %conditional.19 = (bf16[3,256,1792]{2,1,0:T(8,128)(2,1)}, bf16[2,448,28672]{2,1,0:T(8,128)(2,1)}) conditional(s32[]{:T(128)} %bitcast.85, (bf16[256,1792]{1,0:T(8,128)(2,1)}, bf16[256,1792]{1,0:T(8,128)(2,1)}, bf16[256,1792]{1,0:T(8,128)(2,1)}, bf16[2,448,28672]{2,1,0:T(8,128)(2,1)}) %tuple.124, (bf16[256,1792]{1,0:T(8,128)(2,1)}, ...), branch_computations={%region_18.19_spmd, %region_19.20_spmd} | conditional | flops 6579421184 | bytes 33947704 | solution.py:282
  204.2 11.2 %branch_1_fun.9 = bf16[2,448,28672]{2,1,0:T(8,128)(2,1)} custom-call(s32[2]{0:T(128)S(1)} %get-tuple-element.338.cols_ref, bf16[2,448,1024]{2,1,0:T(8,128)(2,1)S(1)} %get-tuple-element.339.left_ref, bf16[256,1792]{1,0:T(8,128)(2,1)S(1)} %get-tuple-element.340.refs_0_, ...), custom_call_target="tpu_custom_call", output_to_operand_aliasing={{}: (10, {})} | custom-call | flops 6576668672 | bytes 17432576 | tf_op jit(solution)/shard_map/cond/branch_1_fun/pallas_call | solution.py:134
  215.5 7.0 %shard_map.19.refs_4_ = bf16[2,448,28672]{2,1,0:T(8,128)(2,1)} custom-call(s32[1]{0:T(128)} %bitcast.71.cols_ref, bf16[2,448,1024]{2,1,0:T(8,128)(2,1)S(1)} %shard_map.17.left_ref, bf16[256,1792]{1,0:T(8,128)(2,1)} %collective-permute-done.25.refs_0_, bf16[3,256,1792]{2,1,0:T(8,128)(2,1)} %get-tuple-element.701.refs_1_, ...), custom_call_target="tpu_custom_call", output_to_operand_aliasing={{}: (6, {})} | custom-call | flops 3288334336 | bytes 8716288 | tf_op jit(solution)/shard_map/pallas_call | solution.py:134
  223.5 6.9 %shard_map.20.refs_12_ = bf16[2,448,28672]{2,1,0:T(8,128)(2,1)} custom-call(s32[1]{0:T(128)} %bitcast.72.cols_ref, bf16[2,448,1024]{2,1,0:T(8,128)(2,1)S(1)} %shard_map.17.left_ref, bf16[256,1792]{1,0:T(8,128)(2,1)} %collective-permute-done.26.refs_0_, bf16[3,256,1792]{2,1,0:T(8,128)(2,1)} %get-tuple-element.701.refs_1_, ...), custom_call_target="tpu_custom_call", output_to_operand_aliasing={{}: (6, {})} | custom-call | flops 3288334336 | bytes 8716288 | tf_op jit(solution)/shard_map/pallas_call | solution.py:134
  232.6 15.2 %shard_map.21 = bf16[2,448,28672]{2,1,0:T(8,128)(2,1)} custom-call(s32[3]{0:T(128)} %copy-done.3, bf16[2,448,1024]{2,1,0:T(8,128)(2,1)S(1)} %shard_map.17.left_ref, bf16[256,1792]{1,0:T(8,128)(2,1)} %collective-permute-done.32.refs_0_, bf16[3,256,1792]{2,1,0:T(8,128)(2,1)} %get-tuple-element.719.refs_1_, ...), custom_call_target="tpu_custom_call", output_to_operand_aliasing={{}: (14, {})} | custom-call | flops 9865003008 | bytes 26148864 | tf_op jit(solution)/shard_map/pallas_call | solution.py:134
  (108 shorter events, 113.5 us)
Async XLA Ops:
  6.4 24.5 %collective-permute-start.12 = (bf16[256,1792]{1,0:T(8,128)(2,1)}, bf16[256,1792]{1,0:T(8,128)(2,1)}, u32[]{:S(2)}, u32[]{:S(2)}) collective-permute-start(bf16[256,1792]{1,0:T(8,128)(2,1)} %get-tuple-element.553.refs_0_), channel_id=1, source_target_pairs={{0,2},{1,3},{2,0},{3,1},{4,6},{5,7},{6,4},{7,5},{8,10},{9,11},{10,... | collective-permute-start | bytes 2752520 | tf_op jit(solution)/shard_map/ppermute | solution.py:257
  9.4 24.0 %collective-permute-start.10 = (bf16[256,1792]{1,0:T(8,128)(2,1)}, bf16[256,1792]{1,0:T(8,128)(2,1)}, u32[]{:S(2)}, u32[]{:S(2)}) collective-permute-start(bf16[256,1792]{1,0:T(8,128)(2,1)} %get-tuple-element.553.refs_0_), channel_id=1, source_target_pairs={{0,8},{1,9},{2,10},{3,11},{4,12},{5,13},{6,14},{7,15},{8,16},{9,17... | collective-permute-start | bytes 2752520 | tf_op jit(solution)/shard_map/ppermute | solution.py:257
  12.4 39.8 %collective-permute-start.17 = (bf16[256,1792]{1,0:T(8,128)(2,1)}, bf16[256,1792]{1,0:T(8,128)(2,1)}, u32[]{:S(2)}, u32[]{:S(2)}) collective-permute-start(bf16[256,1792]{1,0:T(8,128)(2,1)} %get-tuple-element.553.refs_0_), channel_id=1, source_target_pairs={{0,4},{1,5},{2,6},{3,7},{4,0},{5,1},{6,2},{7,3},{8,12},{9,13},{10,... | collective-permute-start | bytes 2752520 | tf_op jit(solution)/shard_map/ppermute | solution.py:257
  18.3 35.4 %collective-permute-start.18 = (bf16[256,1792]{1,0:T(8,128)(2,1)S(1)}, bf16[256,1792]{1,0:T(8,128)(2,1)}, u32[]{:S(2)}, u32[]{:S(2)}) collective-permute-start(bf16[256,1792]{1,0:T(8,128)(2,1)S(1)} %get-tuple-element.554.refs_4_), channel_id=1, source_target_pairs={{0,2},{1,3},{2,0},{3,1},{4,6},{5,7},{6,4},{7,5},{8,10},{9,11},{10,... | collective-permute-start | bytes 2752520 | tf_op jit(solution)/shard_map/ppermute | solution.py:257
  30.8 25.5 %collective-permute-start.16 = (bf16[256,1792]{1,0:T(8,128)(2,1)S(1)}, bf16[256,1792]{1,0:T(8,128)(2,1)}, u32[]{:S(2)}, u32[]{:S(2)}) collective-permute-start(bf16[256,1792]{1,0:T(8,128)(2,1)S(1)} %get-tuple-element.554.refs_4_), channel_id=1, source_target_pairs={{0,8},{1,9},{2,10},{3,11},{4,12},{5,13},{6,14},{7,15},{8,16},{9,17... | collective-permute-start | bytes 2752520 | tf_op jit(solution)/shard_map/ppermute | solution.py:257
  41.7 31.4 %collective-permute-start.13 = (bf16[256,1792]{1,0:T(8,128)(2,1)}, bf16[256,1792]{1,0:T(8,128)(2,1)}, u32[]{:S(2)}, u32[]{:S(2)}) collective-permute-start(bf16[256,1792]{1,0:T(8,128)(2,1)} %collective-permute-done.10), channel_id=1, source_target_pairs={{0,8},{1,9},{2,10},{3,11},{4,12},{5,13},{6,14},{7,15},{8,16},{9,17... | collective-permute-start | bytes 2752520 | tf_op jit(solution)/shard_map/ppermute | solution.py:257
  43.3 29.8 %collective-permute-start.15 = (bf16[256,1792]{1,0:T(8,128)(2,1)}, bf16[256,1792]{1,0:T(8,128)(2,1)}, u32[]{:S(2)}, u32[]{:S(2)}) collective-permute-start(bf16[256,1792]{1,0:T(8,128)(2,1)} %collective-permute-done.11), channel_id=1, source_target_pairs={{0,2},{1,3},{2,0},{3,1},{4,6},{5,7},{6,4},{7,5},{8,10},{9,11},{10,... | collective-permute-start | bytes 2752520 | tf_op jit(solution)/shard_map/ppermute | solution.py:257
  63.7 34.5 %collective-permute-start.24 = (bf16[256,1792]{1,0:T(8,128)(2,1)}, bf16[256,1792]{1,0:T(8,128)(2,1)}, u32[]{:S(2)}, u32[]{:S(2)}) collective-permute-start(bf16[256,1792]{1,0:T(8,128)(2,1)} %collective-permute-done.10), channel_id=1, source_target_pairs={{0,2},{1,3},{2,0},{3,1},{4,6},{5,7},{6,4},{7,5},{8,10},{9,11},{10,... | collective-permute-start | bytes 2752520 | tf_op jit(solution)/shard_map/ppermute | solution.py:257
  65.5 32.8 %collective-permute-start.23 = (bf16[256,1792]{1,0:T(8,128)(2,1)}, bf16[256,1792]{1,0:T(8,128)(2,1)}, u32[]{:S(2)}, u32[]{:S(2)}) collective-permute-start(bf16[256,1792]{1,0:T(8,128)(2,1)} %collective-permute-done.10), channel_id=1, source_target_pairs={{0,4},{1,5},{2,6},{3,7},{4,0},{5,1},{6,2},{7,3},{8,12},{9,13},{10,... | collective-permute-start | bytes 2752520 | tf_op jit(solution)/shard_map/ppermute | solution.py:257
  73.1 23.6 %collective-permute-start.22 = (bf16[256,1792]{1,0:T(8,128)(2,1)}, bf16[256,1792]{1,0:T(8,128)(2,1)}, u32[]{:S(2)}, u32[]{:S(2)}) collective-permute-start(bf16[256,1792]{1,0:T(8,128)(2,1)} %collective-permute-done.16), channel_id=1, source_target_pairs={{0,8},{1,9},{2,10},{3,11},{4,12},{5,13},{6,14},{7,15},{8,16},{9,17... | collective-permute-start | bytes 2752520 | tf_op jit(solution)/shard_map/ppermute | solution.py:257
  94.6 25.3 %collective-permute-start.19 = (bf16[256,1792]{1,0:T(8,128)(2,1)}, bf16[256,1792]{1,0:T(8,128)(2,1)S(1)}, u32[]{:S(2)}, u32[]{:S(2)}) collective-permute-start(bf16[256,1792]{1,0:T(8,128)(2,1)} %collective-permute-done.13), channel_id=1, source_target_pairs={{0,8},{1,9},{2,10},{3,11},{4,12},{5,13},{6,14},{7,15},{8,16},{9,17... | collective-permute-start | bytes 2752520 | tf_op jit(solution)/shard_map/ppermute | solution.py:257
  96.2 25.1 %collective-permute-start.21 = (bf16[256,1792]{1,0:T(8,128)(2,1)}, bf16[256,1792]{1,0:T(8,128)(2,1)}, u32[]{:S(2)}, u32[]{:S(2)}) collective-permute-start(bf16[256,1792]{1,0:T(8,128)(2,1)} %collective-permute-done.16), channel_id=1, source_target_pairs={{0,2},{1,3},{2,0},{3,1},{4,6},{5,7},{6,4},{7,5},{8,10},{9,11},{10,... | collective-permute-start | bytes 2752520 | tf_op jit(solution)/shard_map/ppermute | solution.py:257
  96.7 24.6 %collective-permute-start.20 = (bf16[256,1792]{1,0:T(8,128)(2,1)}, bf16[256,1792]{1,0:T(8,128)(2,1)}, u32[]{:S(2)}, u32[]{:S(2)}) collective-permute-start(bf16[256,1792]{1,0:T(8,128)(2,1)} %collective-permute-done.16), channel_id=1, source_target_pairs={{0,4},{1,5},{2,6},{3,7},{4,0},{5,1},{6,2},{7,3},{8,12},{9,13},{10,... | collective-permute-start | bytes 2752520 | tf_op jit(solution)/shard_map/ppermute | solution.py:257
  111.9 27.7 %collective-permute-start.25 = (bf16[256,1792]{1,0:T(8,128)(2,1)}, bf16[256,1792]{1,0:T(8,128)(2,1)}, u32[]{:S(2)}, u32[]{:S(2)}) collective-permute-start(bf16[256,1792]{1,0:T(8,128)(2,1)} %collective-permute-done.22), channel_id=1, source_target_pairs={{0,8},{1,9},{2,10},{3,11},{4,12},{5,13},{6,14},{7,15},{8,16},{9,17... | collective-permute-start | bytes 2752520 | tf_op jit(solution)/shard_map/ppermute | solution.py:257
  113.5 27.6 %collective-permute-start.27 = (bf16[256,1792]{1,0:T(8,128)(2,1)}, bf16[256,1792]{1,0:T(8,128)(2,1)}, u32[]{:S(2)}, u32[]{:S(2)}) collective-permute-start(bf16[256,1792]{1,0:T(8,128)(2,1)} %collective-permute-done.13), channel_id=1, source_target_pairs={{0,2},{1,3},{2,0},{3,1},{4,6},{5,7},{6,4},{7,5},{8,10},{9,11},{10,... | collective-permute-start | bytes 2752520 | tf_op jit(solution)/shard_map/ppermute | solution.py:257
  128.5 30.0 %collective-permute-start.31 = (bf16[256,1792]{1,0:T(8,128)(2,1)}, bf16[256,1792]{1,0:T(8,128)(2,1)}, u32[]{:S(2)}, u32[]{:S(2)}) collective-permute-start(bf16[256,1792]{1,0:T(8,128)(2,1)} %collective-permute-done.14), channel_id=1, source_target_pairs={{0,8},{1,9},{2,10},{3,11},{4,12},{5,13},{6,14},{7,15},{8,16},{9,17... | collective-permute-start | bytes 2752520 | tf_op jit(solution)/shard_map/ppermute | solution.py:257
  128.5 30.5 %collective-permute-start.33 = (bf16[256,1792]{1,0:T(8,128)(2,1)}, bf16[256,1792]{1,0:T(8,128)(2,1)}, u32[]{:S(2)}, u32[]{:S(2)}) collective-permute-start(bf16[256,1792]{1,0:T(8,128)(2,1)} %collective-permute-done.22), channel_id=1, source_target_pairs={{0,2},{1,3},{2,0},{3,1},{4,6},{5,7},{6,4},{7,5},{8,10},{9,11},{10,... | collective-permute-start | bytes 2752520 | tf_op jit(solution)/shard_map/ppermute | solution.py:257
  154.6 25.3 %collective-permute-start.28 = (bf16[256,1792]{1,0:T(8,128)(2,1)}, bf16[256,1792]{1,0:T(8,128)(2,1)}, u32[]{:S(2)}, u32[]{:S(2)}) collective-permute-start(bf16[256,1792]{1,0:T(8,128)(2,1)} %collective-permute-done.15), channel_id=1, source_target_pairs={{0,8},{1,9},{2,10},{3,11},{4,12},{5,13},{6,14},{7,15},{8,16},{9,17... | collective-permute-start | bytes 2752520 | tf_op jit(solution)/shard_map/ppermute | solution.py:257
  154.7 28.2 %collective-permute-start.29 = (bf16[256,1792]{1,0:T(8,128)(2,1)}, bf16[256,1792]{1,0:T(8,128)(2,1)}, u32[]{:S(2)}, u32[]{:S(2)}) collective-permute-start(bf16[256,1792]{1,0:T(8,128)(2,1)} %collective-permute-done.25.refs_0_), channel_id=1, source_target_pairs={{0,4},{1,5},{2,6},{3,7},{4,0},{5,1},{6,2},{7,3},{8,12},{9,13},{10,... | collective-permute-start | bytes 2752520 | tf_op jit(solution)/shard_map/ppermute | solution.py:257
  158.5 24.4 %collective-permute-start.30 = (bf16[256,1792]{1,0:T(8,128)(2,1)S(1)}, bf16[256,1792]{1,0:T(8,128)(2,1)}, u32[]{:S(2)}, u32[]{:S(2)}) collective-permute-start(bf16[256,1792]{1,0:T(8,128)(2,1)S(1)} %collective-permute-done.19), channel_id=1, source_target_pairs={{0,2},{1,3},{2,0},{3,1},{4,6},{5,7},{6,4},{7,5},{8,10},{9,11},{10,... | collective-permute-start | bytes 2752520 | tf_op jit(solution)/shard_map/ppermute | solution.py:257
  172.4 26.8 %collective-permute-start.37 = (bf16[256,1792]{1,0:T(8,128)(2,1)}, bf16[256,1792]{1,0:T(8,128)(2,1)}, u32[]{:S(2)}, u32[]{:S(2)}) collective-permute-start(bf16[256,1792]{1,0:T(8,128)(2,1)} %collective-permute-done.31), channel_id=1, source_target_pairs={{0,8},{1,9},{2,10},{3,11},{4,12},{5,13},{6,14},{7,15},{8,16},{9,17... | collective-permute-start | bytes 2752520 | tf_op jit(solution)/shard_map/ppermute | solution.py:257
  172.5 27.6 %collective-permute-start.38 = (bf16[256,1792]{1,0:T(8,128)(2,1)S(1)}, bf16[256,1792]{1,0:T(8,128)(2,1)}, u32[]{:S(2)}, u32[]{:S(2)}) collective-permute-start(bf16[256,1792]{1,0:T(8,128)(2,1)S(1)} %collective-permute-done.19), channel_id=1, source_target_pairs={{0,4},{1,5},{2,6},{3,7},{4,0},{5,1},{6,2},{7,3},{8,12},{9,13},{10,... | collective-permute-start | bytes 2752520 | tf_op jit(solution)/shard_map/ppermute | solution.py:257
  196.4 26.0 %collective-permute-start.34 = (bf16[256,1792]{1,0:T(8,128)(2,1)}, bf16[256,1792]{1,0:T(8,128)(2,1)}, u32[]{:S(2)}, u32[]{:S(2)}) collective-permute-start(bf16[256,1792]{1,0:T(8,128)(2,1)} %collective-permute-done.28), channel_id=1, source_target_pairs={{0,8},{1,9},{2,10},{3,11},{4,12},{5,13},{6,14},{7,15},{8,16},{9,17... | collective-permute-start | bytes 2752520 | tf_op jit(solution)/shard_map/ppermute | solution.py:257
  196.5 26.0 %collective-permute-start.35 = (bf16[256,1792]{1,0:T(8,128)(2,1)}, bf16[256,1792]{1,0:T(8,128)(2,1)}, u32[]{:S(2)}, u32[]{:S(2)}) collective-permute-start(bf16[256,1792]{1,0:T(8,128)(2,1)} %collective-permute-done.30), channel_id=1, source_target_pairs={{0,4},{1,5},{2,6},{3,7},{4,0},{5,1},{6,2},{7,3},{8,12},{9,13},{10,... | collective-permute-start | bytes 2752520 | tf_op jit(solution)/shard_map/ppermute | solution.py:257
  (24 other events, 428.2 us)
where the time goes:
time: 249 us; the launch traced here: 248 us
  Pallas kernels  95.2 us (38%)
  waiting for transfers between devices  87.4 us (35%)
  starting transfers between devices  34.6 us (14%)
  other arithmetic  20.8 us (8%)
  local copies, waits for them, and re-layouts  8.51 us (3%)
    pallas_call x9, Pallas kernels, column_blocks(): pl.pallas_call(functools.partial(column_kernel, factor, parts, picks), ou...  92.5 us
    ppermute x30, waiting for transfers between devices, start(): pending[name] = lax.ppermute(mine[source(link, name)], axes, links[link])  62.6 us
    ppermute x30, starting transfers between devices, start(): pending[name] = lax.ppermute(mine[source(link, name)], axes, links[link])  32.8 us
    ppermute x10, waiting for transfers between devices, run(): given = lax.ppermute(jnp.stack(given), axes, cores)  24.8 us
    another operation x10, other arithmetic, run(): given = lax.ppermute(jnp.stack(given), axes, cores)  19.4 us
    slice x1, local copies, waits for them, and re-layouts, meshed(): own = lax.optimization_barrier((acts[:, 0, :], acts[:, 1, :]))  5.2 us
  transfers between devices with their start and end apart: 43, of which 21 were waited for; matrix products, arithmetic and copies ran while one was open for 8% of the time, Pallas kernels for 32%

commit v1 on v0

--- a/solution.py
+++ b/solution.py
@@ -9,7 +9,7 @@
 
 LANES = 128
 KSCALE = 1
-CALLS = (2, 3, 5, 6, 7, 8, 9, 10)
+CALLS = (2, 3, 4, 5, 6, 7, 8, 9, 10)
 VMEM = 56 * 2**20
 
 
@@ -264,25 +264,28 @@
         del todo[: len(now)]
         return [parts_of(near, far) for _, near, far, _ in now]
 
-    def swap(given, groups, out):
+    def swap(given, groups, out, apart=False):
         arrays = [[a for a, _ in g] for g in groups]
         picks = [[at for _, at in g] for g in groups]
 
         def run(given, arrays, out, column, left):
-            given = lax.ppermute(jnp.stack(given), axes, cores)
+            given = list(given) if apart else [jnp.stack(given)]
+            given = [lax.ppermute(a, axes, cores) for a in given]
             if picks:
                 pairs = [list(zip(a, p)) for a, p in zip(arrays, picks)]
                 out = column_blocks(out, left, pairs, column, width, factor)
             return given, out
 
         def skip(given, arrays, out, column, left):
-            return jnp.stack(given), out
+            if picks and out is None:
+                out = jnp.zeros((2, strip, width), given[0].dtype)
+            return list(given) if apart else [jnp.stack(given)], out
 
         column = cols.pop(0) if groups else None
         return lax.cond(cols[-1][0] >= 0, run, skip, given, arrays, out, column, left)
 
     start(0)
-    swapped, _ = swap(list(own), [], None)
+    (swapped,), _ = swap(list(own), [], None)
     start(1)
     for i, step in enumerate(STEPS):
         final = i + 1 == len(STEPS)
@@ -298,20 +301,14 @@
             arrived, cols = lax.optimization_barrier((arrived, cols))
         mine.update(zip(step, arrived))
         if final:
-            for name, a in zip(step, arrived):
-                other[name] = (lax.ppermute(a, axes, cores), None)
-            out = column_blocks(out, left, groups[1:], cols.pop(0), width, factor)
+            swapped, out = swap(arrived, groups[1:], out, apart=True)
+            other.update((name, (a, None)) for name, a in zip(step, swapped))
             break
-        inside = i in CALLS and out is not None
-        swapped, new = swap(arrived, due(i) if inside else [], out if inside else None)
-        if inside:
-            out = new
+        if left is None and i in CALLS:
+            parts = [p for h in range(2) for p in parts_of(("S", 0, h), ("Y", 0, h))]
+            left = left_rows(tok, parts, strip)
+        (swapped,), out = swap(arrived, due(i) if i in CALLS else [], out)
         other.update((name, (swapped, j)) for j, name in enumerate(step))
-        if i in CALLS and not inside:
-            if left is None:
-                parts = [p for h in range(2) for p in parts_of(("S", 0, h), ("Y", 0, h))]
-                left = left_rows(tok, parts, strip)
-            out = column_blocks(out, left, due(i), cols.pop(0), width, factor)
         names = []
         if i + 2 < len(STEPS):
             names = sorted({source(link, name) for link, name in enumerate(STEPS[i + 2])})

time: 249 us -> 240 us (0.964)
  waiting for transfers between devices: 87.4 us -> 82 us
  local copies, waits for them, and re-layouts: 8.51 us -> 5.49 us
  Pallas kernels: 95.2 us -> 97.7 us
    ppermute x13, waiting for transfers between devices: 24.8 us -> 14.4 us  [run(): given = [lax.ppermute(a, axes, cores) for a in given]]
    ppermute x30, waiting for transfers between devices: 62.6 us -> 67.7 us  [start(): pending[name] = lax.ppermute(mine[source(link, name)], axes, links[link])]
    pallas_call x9 -> x10, Pallas kernels: 92.5 us -> 94.9 us  [column_blocks(): pl.pallas_call(functools.partial(column_kernel, factor, parts, picks), ou...]
  transfers between devices with their start and end apart: 43 -> 43, of which waited for: 21 -> 16; matrix products, arithmetic and copies ran while one was open for 8% -> 8% of each run, Pallas kernels for 32% -> 34%
where the time goes in v1:
time: 240 us; the launch traced here: 239 us
  Pallas kernels  97.7 us (41%)
  waiting for transfers between devices  82 us (34%)
  starting transfers between devices  33.5 us (14%)
  other arithmetic  18.8 us (8%)
  local copies, waits for them, and re-layouts  5.49 us (2%)
    pallas_call x10, Pallas kernels, column_blocks(): pl.pallas_call(functools.partial(column_kernel, factor, parts, picks), ou...  94.9 us
    ppermute x30, waiting for transfers between devices, start(): pending[name] = lax.ppermute(mine[source(link, name)], axes, links[link])  67.7 us
    ppermute x30, starting transfers between devices, start(): pending[name] = lax.ppermute(mine[source(link, name)], axes, links[link])  31.7 us
    another operation x10, other arithmetic, run(): given = list(given) if apart else [jnp.stack(given)]  18 us
    ppermute x13, waiting for transfers between devices, run(): given = [lax.ppermute(a, axes, cores) for a in given]  14.4 us
    slice x1, local copies, waits for them, and re-layouts, meshed(): own = lax.optimization_barrier((acts[:, 0, :], acts[:, 1, :]))  5.2 us
  transfers between devices with their start and end apart: 43, of which 16 were waited for; matrix products, arithmetic and copies ran while one was open for 8% of the time, Pallas kernels for 34%

profile of v1, /device:TPU:0, one launch (start us, length us, event | category | flops | bytes accessed | tf_op | source)
XLA Modules:
  0.0 239.1 jit_solution(12714170846885704897)
XLA Ops:
  18.7 13.2 %collective-permute-done.13 = bf16[256,1792]{1,0:T(8,128)(2,1)} collective-permute-done((bf16[256,1792]{1,0:T(8,128)(2,1)S(1)}, bf16[256,1792]{1,0:T(8,128)(2,1)}, u32[]{:S(2)}, u32[]{:S(2)}) %collective-permute-start.13) | collective-permute-done | bytes 917536 | tf_op jit(solution)/shard_map/ppermute | solution.py:257
  33.7 7.3 %conditional.12 = (bf16[3,256,1792]{2,1,0:T(8,128)(2,1)}) conditional(s32[]{:T(128)} %bitcast.76, (bf16[256,1792]{1,0:T(8,128)(2,1)}, bf16[256,1792]{1,0:T(8,128)(2,1)}, bf16[256,1792]{1,0:T(8,128)(2,1)}) %tuple.107, (bf16[256,1792]{1,0:T(8,128)(2,1)}, bf16[256,1792]{1,0:T(8,128)(2,1)}, bf16[256,1792]{1,0:T(8,128)(2,1)}) %tuple.107), branch_computations={%region_2.3_spmd, %region_3.4_spmd} | conditional | flops 2752512 | bytes 16515120 | solution.py:285
  42.5 9.0 %collective-permute-done.19 = bf16[256,1792]{1,0:T(8,128)(2,1)} collective-permute-done((bf16[256,1792]{1,0:T(8,128)(2,1)S(1)}, bf16[256,1792]{1,0:T(8,128)(2,1)}, u32[]{:S(2)}, u32[]{:S(2)}) %collective-permute-start.19) | collective-permute-done | bytes 917536 | tf_op jit(solution)/shard_map/ppermute | solution.py:257
  53.3 7.3 %conditional.13 = (bf16[3,256,1792]{2,1,0:T(8,128)(2,1)}) conditional(s32[]{:T(128)} %bitcast.77, (bf16[256,1792]{1,0:T(8,128)(2,1)}, bf16[256,1792]{1,0:T(8,128)(2,1)}, bf16[256,1792]{1,0:T(8,128)(2,1)}) %tuple.110, (bf16[256,1792]{1,0:T(8,128)(2,1)}, bf16[256,1792]{1,0:T(8,128)(2,1)}, bf16[256,1792]{1,0:T(8,128)(2,1)}) %tuple.110), branch_computations={%region_4.5_spmd, %region_5.6_spmd} | conditional | flops 2752512 | bytes 16515120 | solution.py:285
  62.2 8.9 %collective-permute-done.16 = bf16[256,1792]{1,0:T(8,128)(2,1)S(1)} collective-permute-done((bf16[256,1792]{1,0:T(8,128)(2,1)}, bf16[256,1792]{1,0:T(8,128)(2,1)S(1)}, u32[]{:S(2)}, u32[]{:S(2)}) %collective-permute-start.16) | collective-permute-done | bytes 917536 | tf_op jit(solution)/shard_map/ppermute | solution.py:257
  75.7 13.1 %conditional.14 = (bf16[3,256,1792]{2,1,0:T(8,128)(2,1)}, bf16[2,448,28672]{2,1,0:T(8,128)(2,1)}) conditional(s32[]{:T(128)} %bitcast.78, (bf16[256,1792]{1,0:T(8,128)(2,1)S(1)}, bf16[256,1792]{1,0:T(8,128)(2,1)}, bf16[256,1792]{1,0:T(8,128)(2,1)}) %tuple.172, (bf16[256,1792]{1,0:T(8,128)(2,1)S(1)}, bf16[256,1792]{1,0:T(8,128)(2,1)}, ...), branch_computations={%region_6.7_spmd, %region_7.8_spmd} | conditional | flops 6579421184 | bytes 56885264 | solution.py:285
  77.6 11.2 %branch_1_fun.8 = bf16[2,448,28672]{2,1,0:T(8,128)(2,1)} custom-call(s32[2]{0:T(128)S(1)} %get-tuple-element.308.cols_ref, bf16[2,448,1024]{2,1,0:T(8,128)(2,1)S(1)} %get-tuple-element.309.left_ref, bf16[256,1792]{1,0:T(8,128)(2,1)S(1)} %get-tuple-element.310.refs_0_, bf16[2,256,1792]{2,1,0:T(8,128)(2,1)} %get-tuple-element.311.refs_1_.refs_5_, ...), custom_call_target="tpu_custom_call" | custom-call | flops 6576668672 | bytes 17432576 | tf_op jit(solution)/shard_map/cond/branch_1_fun/pallas_call | solution.py:134
  92.3 13.6 %conditional.15 = (bf16[3,256,1792]{2,1,0:T(8,128)(2,1)}, bf16[2,448,28672]{2,1,0:T(8,128)(2,1)}) conditional(s32[]{:T(128)} %bitcast.80, (bf16[256,1792]{1,0:T(8,128)(2,1)}, bf16[256,1792]{1,0:T(8,128)(2,1)}, bf16[256,1792]{1,0:T(8,128)(2,1)}, bf16[2,448,28672]{2,1,0:T(8,128)(2,1)}) %tuple.117, (bf16[256,1792]{1,0:T(8,128)(2,1)}, ...), branch_computations={%region_8.9_spmd, %region_9.10_spmd} | conditional | flops 6579421184 | bytes 33947704 | solution.py:285
  94.6 11.3 %branch_1_fun.9 = bf16[2,448,28672]{2,1,0:T(8,128)(2,1)} custom-call(s32[2]{0:T(128)S(1)} %get-tuple-element.324.cols_ref, bf16[2,448,1024]{2,1,0:T(8,128)(2,1)S(1)} %get-tuple-element.325.left_ref, bf16[256,1792]{1,0:T(8,128)(2,1)} %get-tuple-element.326.refs_0_, bf16[3,256,1792]{2,1,0:T(8,128)(2,1)} %get-tuple-element.327.refs_1_, ...), custom_call_target="tpu_custom_call", output_to_operand_aliasing={{}: (10, {})} | custom-call | flops 6576668672 | bytes 17432576 | tf_op jit(solution)/shard_map/cond/branch_1_fun/pallas_call | solution.py:134
  107.3 6.9 %collective-permute-done.22 = bf16[256,1792]{1,0:T(8,128)(2,1)} collective-permute-done((bf16[256,1792]{1,0:T(8,128)(2,1)}, bf16[256,1792]{1,0:T(8,128)(2,1)}, u32[]{:S(2)}, u32[]{:S(2)}) %collective-permute-start.22) | collective-permute-done | bytes 917536 | tf_op jit(solution)/shard_map/ppermute | solution.py:257
  115.1 9.1 %conditional.16 = (bf16[3,256,1792]{2,1,0:T(8,128)(2,1)}, bf16[2,448,28672]{2,1,0:T(8,128)(2,1)}) conditional(s32[]{:T(128)} %bitcast.81, (bf16[256,1792]{1,0:T(8,128)(2,1)}, bf16[256,1792]{1,0:T(8,128)(2,1)}, bf16[256,1792]{1,0:T(8,128)(2,1)}, bf16[2,448,28672]{2,1,0:T(8,128)(2,1)}) %tuple.121, (bf16[256,1792]{1,0:T(8,128)(2,1)}, ...), branch_computations={%region_10.11_spmd, %region_11.12_spmd} | conditional | flops 3291086848 | bytes 25231416 | solution.py:285
  117.3 7.0 %branch_1_fun.10 = bf16[2,448,28672]{2,1,0:T(8,128)(2,1)} custom-call(s32[1]{0:T(128)} %get-tuple-element.341.cols_ref, bf16[2,448,1024]{2,1,0:T(8,128)(2,1)S(1)} %get-tuple-element.342.left_ref, bf16[256,1792]{1,0:T(8,128)(2,1)} %get-tuple-element.343.refs_0_, bf16[3,256,1792]{2,1,0:T(8,128)(2,1)} %get-tuple-element.344.refs_1_, ...), custom_call_target="tpu_custom_call", output_to_operand_aliasing={{}: (6, {})} | custom-call | flops 3288334336 | bytes 8716288 | tf_op jit(solution)/shard_map/cond/branch_1_fun/pallas_call | solution.py:134
  125.9 7.9 %collective-permute-done.28.refs_0_ = bf16[256,1792]{1,0:T(8,128)(2,1)} collective-permute-done((bf16[256,1792]{1,0:T(8,128)(2,1)}, bf16[256,1792]{1,0:T(8,128)(2,1)}, u32[]{:S(2)}, u32[]{:S(2)}) %collective-permute-start.28) | collective-permute-done | bytes 917536 | tf_op jit(solution)/shard_map/ppermute | solution.py:257
  136.1 8.8 %conditional.17 = (bf16[3,256,1792]{2,1,0:T(8,128)(2,1)}, bf16[2,448,28672]{2,1,0:T(8,128)(2,1)}) conditional(s32[]{:T(128)} %bitcast.82, (bf16[256,1792]{1,0:T(8,128)(2,1)}, bf16[256,1792]{1,0:T(8,128)(2,1)S(1)}, bf16[256,1792]{1,0:T(8,128)(2,1)}, bf16[2,448,28672]{2,1,0:T(8,128)(2,1)}) %tuple.125, (bf16[256,1792]{1,0:T(8,128)(2,1)}, ...), branch_computations={%region_12.13_spmd, %region_13.14_spmd} | conditional | flops 3291086848 | bytes 25231416 | solution.py:285
  137.9 7.0 %branch_1_fun.11 = bf16[2,448,28672]{2,1,0:T(8,128)(2,1)} custom-call(s32[1]{0:T(128)} %get-tuple-element.355.cols_ref, bf16[2,448,1024]{2,1,0:T(8,128)(2,1)S(1)} %get-tuple-element.356.left_ref, bf16[256,1792]{1,0:T(8,128)(2,1)} %get-tuple-element.357.refs_0_, bf16[3,256,1792]{2,1,0:T(8,128)(2,1)} %get-tuple-element.358.refs_1_, ...), custom_call_target="tpu_custom_call", output_to_operand_aliasing={{}: (6, {})} | custom-call | flops 3288334336 | bytes 8716288 | tf_op jit(solution)/shard_map/cond/branch_1_fun/pallas_call | solution.py:134
  146.5 7.0 %collective-permute-done.34 = bf16[256,1792]{1,0:T(8,128)(2,1)} collective-permute-done((bf16[256,1792]{1,0:T(8,128)(2,1)}, bf16[256,1792]{1,0:T(8,128)(2,1)}, u32[]{:S(2)}, u32[]{:S(2)}) %collective-permute-start.34) | collective-permute-done | bytes 917536 | tf_op jit(solution)/shard_map/ppermute | solution.py:257
  155.8 9.1 %conditional.18 = (bf16[3,256,1792]{2,1,0:T(8,128)(2,1)}, bf16[2,448,28672]{2,1,0:T(8,128)(2,1)}) conditional(s32[]{:T(128)} %bitcast.83, (bf16[256,1792]{1,0:T(8,128)(2,1)}, bf16[256,1792]{1,0:T(8,128)(2,1)}, bf16[256,1792]{1,0:T(8,128)(2,1)}, bf16[2,448,28672]{2,1,0:T(8,128)(2,1)}) %tuple.129, (bf16[256,1792]{1,0:T(8,128)(2,1)}, ...), branch_computations={%region_14.15_spmd, %region_15.16_spmd} | conditional | flops 3291086848 | bytes 28901460 | solution.py:285
  175.4 13.4 %conditional.19 = (bf16[3,256,1792]{2,1,0:T(8,128)(2,1)}, bf16[2,448,28672]{2,1,0:T(8,128)(2,1)}) conditional(s32[]{:T(128)} %bitcast.84, (bf16[256,1792]{1,0:T(8,128)(2,1)}, bf16[256,1792]{1,0:T(8,128)(2,1)}, bf16[256,1792]{1,0:T(8,128)(2,1)}, bf16[2,448,28672]{2,1,0:T(8,128)(2,1)}) %tuple.133, (bf16[256,1792]{1,0:T(8,128)(2,1)}, ...), branch_computations={%region_16.17_spmd, %region_17.18_spmd} | conditional | flops 6579421184 | bytes 33947704 | solution.py:285
  177.6 11.3 %branch_1_fun.13 = bf16[2,448,28672]{2,1,0:T(8,128)(2,1)} custom-call(s32[2]{0:T(128)S(1)} %get-tuple-element.383.cols_ref, bf16[2,448,1024]{2,1,0:T(8,128)(2,1)S(1)} %get-tuple-element.384.left_ref, bf16[256,1792]{1,0:T(8,128)(2,1)} %get-tuple-element.385.refs_0_, ...), custom_call_target="tpu_custom_call", output_to_operand_aliasing={{}: (10, {})} | custom-call | flops 6576668672 | bytes 17432576 | tf_op jit(solution)/shard_map/cond/branch_1_fun/pallas_call | solution.py:134
  195.1 13.6 %conditional.20 = (bf16[3,256,1792]{2,1,0:T(8,128)(2,1)}, bf16[2,448,28672]{2,1,0:T(8,128)(2,1)}) conditional(s32[]{:T(128)} %bitcast.85, (bf16[256,1792]{1,0:T(8,128)(2,1)}, bf16[256,1792]{1,0:T(8,128)(2,1)}, bf16[256,1792]{1,0:T(8,128)(2,1)}, bf16[2,448,28672]{2,1,0:T(8,128)(2,1)}) %tuple.137, (bf16[256,1792]{1,0:T(8,128)(2,1)}, ...), branch_computations={%region_18.19_spmd, %region_19.20_spmd} | conditional | flops 6579421184 | bytes 33947704 | solution.py:285
  197.4 11.3 %branch_1_fun.14 = bf16[2,448,28672]{2,1,0:T(8,128)(2,1)} custom-call(s32[2]{0:T(128)S(1)} %get-tuple-element.399.cols_ref, bf16[2,448,1024]{2,1,0:T(8,128)(2,1)S(1)} %get-tuple-element.400.left_ref, bf16[256,1792]{1,0:T(8,128)(2,1)} %get-tuple-element.401.refs_0_, ...), custom_call_target="tpu_custom_call", output_to_operand_aliasing={{}: (10, {})} | custom-call | flops 6576668672 | bytes 17432576 | tf_op jit(solution)/shard_map/cond/branch_1_fun/pallas_call | solution.py:134
  208.7 7.0 %shard_map.18 = bf16[2,448,28672]{2,1,0:T(8,128)(2,1)} custom-call(s32[1]{0:T(128)} %bitcast.71.cols_ref, bf16[2,448,1024]{2,1,0:T(8,128)(2,1)S(1)} %shard_map.17.left_ref, bf16[256,1792]{1,0:T(8,128)(2,1)} %collective-permute-done.28.refs_0_, bf16[3,256,1792]{2,1,0:T(8,128)(2,1)} %get-tuple-element.802.refs_1_, ...), custom_call_target="tpu_custom_call", output_to_operand_aliasing={{}: (6, {})} | custom-call | flops 3288334336 | bytes 8716288 | tf_op jit(solution)/shard_map/pallas_call | solution.py:134
  215.8 8.0 %conditional.21 = (bf16[256,1792]{1,0:T(8,128)(2,1)}, bf16[256,1792]{1,0:T(8,128)(2,1)}, bf16[256,1792]{1,0:T(8,128)(2,1)}, bf16[2,448,28672]{2,1,0:T(8,128)(2,1)}) conditional(s32[]{:T(128)} %bitcast.86, (bf16[256,1792]{1,0:T(8,128)(2,1)}, bf16[256,1792]{1,0:T(8,128)(2,1)}, bf16[256,1792]{1,0:T(8,128)(2,1)}, ...), branch_computations={%region_20.21_spmd, %region_21.22_spmd} | conditional | flops 3288334336 | bytes 19726488 | solution.py:285
  223.7 15.2 %shard_map.19 = bf16[2,448,28672]{2,1,0:T(8,128)(2,1)} custom-call(s32[3]{0:T(128)} %copy-done.5, bf16[2,448,1024]{2,1,0:T(8,128)(2,1)S(1)} %shard_map.17.left_ref, bf16[256,1792]{1,0:T(8,128)(2,1)} %collective-permute-done.35.refs_0_, bf16[3,256,1792]{2,1,0:T(8,128)(2,1)} %get-tuple-element.820.refs_1_, ...), custom_call_target="tpu_custom_call", output_to_operand_aliasing={{}: (14, {})} | custom-call | flops 9865003008 | bytes 26148864 | tf_op jit(solution)/shard_map/pallas_call | solution.py:134
  (115 shorter events, 107.6 us)
Async XLA Ops:
  5.5 26.4 %collective-permute-start.13 = (bf16[256,1792]{1,0:T(8,128)(2,1)S(1)}, bf16[256,1792]{1,0:T(8,128)(2,1)}, u32[]{:S(2)}, u32[]{:S(2)}) collective-permute-start(bf16[256,1792]{1,0:T(8,128)(2,1)S(1)} %get-tuple-element.641.refs_0_), channel_id=1, source_target_pairs={{0,8},{1,9},{2,10},{3,11},{4,12},{5,13},{6,14},{7,15},{8,16},{9,17... | collective-permute-start | bytes 2752520 | tf_op jit(solution)/shard_map/ppermute | solution.py:257
  8.6 25.1 %collective-permute-start.14 = (bf16[256,1792]{1,0:T(8,128)(2,1)S(1)}, bf16[256,1792]{1,0:T(8,128)(2,1)}, u32[]{:S(2)}, u32[]{:S(2)}) collective-permute-start(bf16[256,1792]{1,0:T(8,128)(2,1)S(1)} %get-tuple-element.642.refs_4_), channel_id=1, source_target_pairs={{0,4},{1,5},{2,6},{3,7},{4,0},{5,1},{6,2},{7,3},{8,12},{9,13},{10,... | collective-permute-start | bytes 2752520 | tf_op jit(solution)/shard_map/ppermute | solution.py:257
  10.0 23.6 %collective-permute-start.15 = (bf16[256,1792]{1,0:T(8,128)(2,1)S(1)}, bf16[256,1792]{1,0:T(8,128)(2,1)}, u32[]{:S(2)}, u32[]{:S(2)}) collective-permute-start(bf16[256,1792]{1,0:T(8,128)(2,1)S(1)} %get-tuple-element.641.refs_0_), channel_id=1, source_target_pairs={{0,2},{1,3},{2,0},{3,1},{4,6},{5,7},{6,4},{7,5},{8,10},{9,11},{10,... | collective-permute-start | bytes 2752520 | tf_op jit(solution)/shard_map/ppermute | solution.py:257
  11.6 40.0 %collective-permute-start.19 = (bf16[256,1792]{1,0:T(8,128)(2,1)S(1)}, bf16[256,1792]{1,0:T(8,128)(2,1)}, u32[]{:S(2)}, u32[]{:S(2)}) collective-permute-start(bf16[256,1792]{1,0:T(8,128)(2,1)S(1)} %get-tuple-element.642.refs_4_), channel_id=1, source_target_pairs={{0,8},{1,9},{2,10},{3,11},{4,12},{5,13},{6,14},{7,15},{8,16},{9,17... | collective-permute-start | bytes 2752520 | tf_op jit(solution)/shard_map/ppermute | solution.py:257
  17.3 36.0 %collective-permute-start.20 = (bf16[256,1792]{1,0:T(8,128)(2,1)S(1)}, bf16[256,1792]{1,0:T(8,128)(2,1)}, u32[]{:S(2)}, u32[]{:S(2)}) collective-permute-start(bf16[256,1792]{1,0:T(8,128)(2,1)S(1)} %get-tuple-element.641.refs_0_), channel_id=1, source_target_pairs={{0,4},{1,5},{2,6},{3,7},{4,0},{5,1},{6,2},{7,3},{8,12},{9,13},{10,... | collective-permute-start | bytes 2752520 | tf_op jit(solution)/shard_map/ppermute | solution.py:257
  41.0 30.1 %collective-permute-start.16 = (bf16[256,1792]{1,0:T(8,128)(2,1)}, bf16[256,1792]{1,0:T(8,128)(2,1)S(1)}, u32[]{:S(2)}, u32[]{:S(2)}) collective-permute-start(bf16[256,1792]{1,0:T(8,128)(2,1)} %collective-permute-done.13), channel_id=1, source_target_pairs={{0,8},{1,9},{2,10},{3,11},{4,12},{5,13},{6,14},{7,15},{8,16},{9,17... | collective-permute-start | bytes 2752520 | tf_op jit(solution)/shard_map/ppermute | solution.py:257
  41.4 34.2 %collective-permute-start.17 = (bf16[256,1792]{1,0:T(8,128)(2,1)}, bf16[256,1792]{1,0:T(8,128)(2,1)}, u32[]{:S(2)}, u32[]{:S(2)}) collective-permute-start(bf16[256,1792]{1,0:T(8,128)(2,1)} %collective-permute-done.15.refs_2_), channel_id=1, source_target_pairs={{0,4},{1,5},{2,6},{3,7},{4,0},{5,1},{6,2},{7,3},{8,12},{9,13},{10,... | collective-permute-start | bytes 2752520 | tf_op jit(solution)/shard_map/ppermute | solution.py:257
  51.5 24.1 %collective-permute-start.18 = (bf16[256,1792]{1,0:T(8,128)(2,1)}, bf16[256,1792]{1,0:T(8,128)(2,1)}, u32[]{:S(2)}, u32[]{:S(2)}) collective-permute-start(bf16[256,1792]{1,0:T(8,128)(2,1)} %collective-permute-done.14), channel_id=1, source_target_pairs={{0,2},{1,3},{2,0},{3,1},{4,6},{5,7},{6,4},{7,5},{8,10},{9,11},{10,... | collective-permute-start | bytes 2752520 | tf_op jit(solution)/shard_map/ppermute | solution.py:257
  60.7 29.8 %collective-permute-start.25 = (bf16[256,1792]{1,0:T(8,128)(2,1)}, bf16[256,1792]{1,0:T(8,128)(2,1)}, u32[]{:S(2)}, u32[]{:S(2)}) collective-permute-start(bf16[256,1792]{1,0:T(8,128)(2,1)} %collective-permute-done.19), channel_id=1, source_target_pairs={{0,8},{1,9},{2,10},{3,11},{4,12},{5,13},{6,14},{7,15},{8,16},{9,17... | collective-permute-start | bytes 2752520 | tf_op jit(solution)/shard_map/ppermute | solution.py:257
  60.9 30.7 %collective-permute-start.26 = (bf16[256,1792]{1,0:T(8,128)(2,1)}, bf16[256,1792]{1,0:T(8,128)(2,1)}, u32[]{:S(2)}, u32[]{:S(2)}) collective-permute-start(bf16[256,1792]{1,0:T(8,128)(2,1)} %collective-permute-done.13), channel_id=1, source_target_pairs={{0,4},{1,5},{2,6},{3,7},{4,0},{5,1},{6,2},{7,3},{8,12},{9,13},{10,... | collective-permute-start | bytes 2752520 | tf_op jit(solution)/shard_map/ppermute | solution.py:257
  88.8 25.3 %collective-permute-start.22 = (bf16[256,1792]{1,0:T(8,128)(2,1)}, bf16[256,1792]{1,0:T(8,128)(2,1)}, u32[]{:S(2)}, u32[]{:S(2)}) collective-permute-start(bf16[256,1792]{1,0:T(8,128)(2,1)} %copy-done.2), channel_id=1, source_target_pairs={{0,8},{1,9},{2,10},{3,11},{4,12},{5,13},{6,14},{7,15},{8,16},{9,17... | collective-permute-start | bytes 2752520 | tf_op jit(solution)/shard_map/ppermute | solution.py:257
  88.9 26.2 %collective-permute-start.23 = (bf16[256,1792]{1,0:T(8,128)(2,1)}, bf16[256,1792]{1,0:T(8,128)(2,1)}, u32[]{:S(2)}, u32[]{:S(2)}) collective-permute-start(bf16[256,1792]{1,0:T(8,128)(2,1)} %collective-permute-done.19), channel_id=1, source_target_pairs={{0,4},{1,5},{2,6},{3,7},{4,0},{5,1},{6,2},{7,3},{8,12},{9,13},{10,... | collective-permute-start | bytes 2752520 | tf_op jit(solution)/shard_map/ppermute | solution.py:257
  90.5 24.6 %collective-permute-start.24 = (bf16[256,1792]{1,0:T(8,128)(2,1)}, bf16[256,1792]{1,0:T(8,128)(2,1)}, u32[]{:S(2)}, u32[]{:S(2)}) collective-permute-start(bf16[256,1792]{1,0:T(8,128)(2,1)} %collective-permute-done.19), channel_id=1, source_target_pairs={{0,2},{1,3},{2,0},{3,1},{4,6},{5,7},{6,4},{7,5},{8,10},{9,11},{10,... | collective-permute-start | bytes 2752520 | tf_op jit(solution)/shard_map/ppermute | solution.py:257
  105.9 27.9 %collective-permute-start.28 = (bf16[256,1792]{1,0:T(8,128)(2,1)}, bf16[256,1792]{1,0:T(8,128)(2,1)}, u32[]{:S(2)}, u32[]{:S(2)}) collective-permute-start(bf16[256,1792]{1,0:T(8,128)(2,1)} %collective-permute-done.25), channel_id=1, source_target_pairs={{0,8},{1,9},{2,10},{3,11},{4,12},{5,13},{6,14},{7,15},{8,16},{9,17... | collective-permute-start | bytes 2752520 | tf_op jit(solution)/shard_map/ppermute | solution.py:257
  106.4 28.3 %collective-permute-start.29 = (bf16[256,1792]{1,0:T(8,128)(2,1)}, bf16[256,1792]{1,0:T(8,128)(2,1)S(1)}, u32[]{:S(2)}, u32[]{:S(2)}) collective-permute-start(bf16[256,1792]{1,0:T(8,128)(2,1)} %copy-done.2), channel_id=1, source_target_pairs={{0,4},{1,5},{2,6},{3,7},{4,0},{5,1},{6,2},{7,3},{8,12},{9,13},{10,... | collective-permute-start | bytes 2752520 | tf_op jit(solution)/shard_map/ppermute | solution.py:257
  124.2 29.2 %collective-permute-start.34 = (bf16[256,1792]{1,0:T(8,128)(2,1)}, bf16[256,1792]{1,0:T(8,128)(2,1)}, u32[]{:S(2)}, u32[]{:S(2)}) collective-permute-start(bf16[256,1792]{1,0:T(8,128)(2,1)} %collective-permute-done.17), channel_id=1, source_target_pairs={{0,8},{1,9},{2,10},{3,11},{4,12},{5,13},{6,14},{7,15},{8,16},{9,17... | collective-permute-start | bytes 2752520 | tf_op jit(solution)/shard_map/ppermute | solution.py:257
  124.3 30.1 %collective-permute-start.35 = (bf16[256,1792]{1,0:T(8,128)(2,1)}, bf16[256,1792]{1,0:T(8,128)(2,1)}, u32[]{:S(2)}, u32[]{:S(2)}) collective-permute-start(bf16[256,1792]{1,0:T(8,128)(2,1)} %collective-permute-done.25), channel_id=1, source_target_pairs={{0,4},{1,5},{2,6},{3,7},{4,0},{5,1},{6,2},{7,3},{8,12},{9,13},{10,... | collective-permute-start | bytes 2752520 | tf_op jit(solution)/shard_map/ppermute | solution.py:257
  144.9 28.2 %collective-permute-start.31 = (bf16[256,1792]{1,0:T(8,128)(2,1)}, bf16[256,1792]{1,0:T(8,128)(2,1)}, u32[]{:S(2)}, u32[]{:S(2)}) collective-permute-start(bf16[256,1792]{1,0:T(8,128)(2,1)} %collective-permute-done.18), channel_id=1, source_target_pairs={{0,8},{1,9},{2,10},{3,11},{4,12},{5,13},{6,14},{7,15},{8,16},{9,17... | collective-permute-start | bytes 2752520 | tf_op jit(solution)/shard_map/ppermute | solution.py:257
  145.0 29.1 %collective-permute-start.32 = (bf16[256,1792]{1,0:T(8,128)(2,1)}, bf16[256,1792]{1,0:T(8,128)(2,1)}, u32[]{:S(2)}, u32[]{:S(2)}) collective-permute-start(bf16[256,1792]{1,0:T(8,128)(2,1)} %collective-permute-done.28.refs_0_), channel_id=1, source_target_pairs={{0,4},{1,5},{2,6},{3,7},{4,0},{5,1},{6,2},{7,3},{8,12},{9,13},{10,... | collective-permute-start | bytes 2752520 | tf_op jit(solution)/shard_map/ppermute | solution.py:257
  164.9 27.5 %collective-permute-start.40 = (bf16[256,1792]{1,0:T(8,128)(2,1)}, bf16[256,1792]{1,0:T(8,128)(2,1)}, u32[]{:S(2)}, u32[]{:S(2)}) collective-permute-start(bf16[256,1792]{1,0:T(8,128)(2,1)} %collective-permute-done.34), channel_id=1, source_target_pairs={{0,8},{1,9},{2,10},{3,11},{4,12},{5,13},{6,14},{7,15},{8,16},{9,17... | collective-permute-start | bytes 2752520 | tf_op jit(solution)/shard_map/ppermute | solution.py:257
  165.0 28.4 %collective-permute-start.41 = (bf16[256,1792]{1,0:T(8,128)(2,1)}, bf16[256,1792]{1,0:T(8,128)(2,1)}, u32[]{:S(2)}, u32[]{:S(2)}) collective-permute-start(bf16[256,1792]{1,0:T(8,128)(2,1)} %collective-permute-done.22), channel_id=1, source_target_pairs={{0,4},{1,5},{2,6},{3,7},{4,0},{5,1},{6,2},{7,3},{8,12},{9,13},{10,... | collective-permute-start | bytes 2752520 | tf_op jit(solution)/shard_map/ppermute | solution.py:257
  188.9 26.8 %collective-permute-start.37 = (bf16[256,1792]{1,0:T(8,128)(2,1)}, bf16[256,1792]{1,0:T(8,128)(2,1)}, u32[]{:S(2)}, u32[]{:S(2)}) collective-permute-start(bf16[256,1792]{1,0:T(8,128)(2,1)} %collective-permute-done.31), channel_id=1, source_target_pairs={{0,8},{1,9},{2,10},{3,11},{4,12},{5,13},{6,14},{7,15},{8,16},{9,17... | collective-permute-start | bytes 2752520 | tf_op jit(solution)/shard_map/ppermute | solution.py:257
  188.9 26.8 %collective-permute-start.38 = (bf16[256,1792]{1,0:T(8,128)(2,1)}, bf16[256,1792]{1,0:T(8,128)(2,1)}, u32[]{:S(2)}, u32[]{:S(2)}) collective-permute-start(bf16[256,1792]{1,0:T(8,128)(2,1)} %collective-permute-done.33), channel_id=1, source_target_pairs={{0,4},{1,5},{2,6},{3,7},{4,0},{5,1},{6,2},{7,3},{8,12},{9,13},{10,... | collective-permute-start | bytes 2752520 | tf_op jit(solution)/shard_map/ppermute | solution.py:257
  192.4 23.3 %collective-permute-start.39 = (bf16[256,1792]{1,0:T(8,128)(2,1)}, bf16[256,1792]{1,0:T(8,128)(2,1)}, u32[]{:S(2)}, u32[]{:S(2)}) collective-permute-start(bf16[256,1792]{1,0:T(8,128)(2,1)} %collective-permute-done.32.refs_8_), channel_id=1, source_target_pairs={{0,2},{1,3},{2,0},{3,1},{4,6},{5,7},{6,4},{7,5},{8,10},{9,11},{10,... | collective-permute-start | bytes 2752520 | tf_op jit(solution)/shard_map/ppermute | solution.py:257
  (27 other events, 492.5 us)

commit v2 on v1

--- a/solution.py
+++ b/solution.py
@@ -170,10 +170,10 @@
 
 
 STEPS = [
-    (("S", 1, 0), ("X", 0, 1), ("Y", 0, 0)),
-    (("S", 1, 1), ("X", 0, 0), ("Y", 0, 1)),
-    (("S", 2, 0), ("D", 0, 0), ("D", 0, 1)),
-    (("S", 2, 1), ("X", 1, 0), ("Y", 1, 0)),
+    (("S", 1, 0), ("X", 0, 0), ("Y", 0, 0)),
+    (("S", 1, 1), ("X", 0, 1), ("Y", 0, 1)),
+    (("S", 2, 0), ("D", 0, 0), ("Y", 1, 0)),
+    (("S", 2, 1), ("X", 1, 0), ("D", 0, 1)),
     (("S", 3, 0), ("X", 1, 1), ("Y", 1, 1)),
     (("S", 3, 1), ("X", 2, 0), ("Y", 2, 0)),
     (("D", 1, 0), ("X", 2, 1), ("Y", 2, 1)),
@@ -227,7 +227,8 @@
             cols += [2 * zk + xk, 2 * nblk - 1 - (2 * zk + xk)]
     cols = [c.astype(jnp.int32) for c in cols]
 
-    own = lax.optimization_barrier((acts[:, 0, :], acts[:, 1, :]))
+    first, acts = lax.optimization_barrier((acts[:, 0, :], acts))
+    own = (first, lax.optimization_barrier(acts[:, 1, :]))
     mine = {("S", 0, 0): own[0], ("S", 0, 1): own[1]}
     other = {}
     ready = {("S", 0, 0): 0, ("S", 0, 1): 0}

time: 240 us -> 237 us (0.988)
  local copies, waits for them, and re-layouts: 5.49 us -> 2.93 us
    slice x1 -> x0, local copies, waits for them, and re-layouts: 5.2 us -> none  [meshed(): own = lax.optimization_barrier((acts[:, 0, :], acts[:, 1, :]))]
    unnamed x14 -> x13, local copies, waits for them, and re-layouts: 0.03 us -> 2.68 us
  transfers between devices with their start and end apart: 43 -> 43, of which waited for: 16 -> 16; matrix products, arithmetic and copies ran while one was open for 8% -> 9% of each run, Pallas kernels for 34% -> 35%
where the time goes in v2:
time: 237 us; the launch traced here: 236 us
  Pallas kernels  97.7 us (41%)
  waiting for transfers between devices  80.8 us (34%)
  starting transfers between devices  33.7 us (14%)
  other arithmetic  19.9 us (8%)
  local copies, waits for them, and re-layouts  2.93 us (1%)
    pallas_call x10, Pallas kernels, column_blocks(): pl.pallas_call(functools.partial(column_kernel, factor, parts, picks), ou...  94.9 us
    ppermute x30, waiting for transfers between devices, start(): pending[name] = lax.ppermute(mine[source(link, name)], axes, links[link])  66.4 us
    ppermute x30, starting transfers between devices, start(): pending[name] = lax.ppermute(mine[source(link, name)], axes, links[link])  31.9 us
    another operation x10, other arithmetic, run(): given = list(given) if apart else [jnp.stack(given)]  19.2 us
    ppermute x13, waiting for transfers between devices, run(): given = [lax.ppermute(a, axes, cores) for a in given]  14.4 us
  transfers between devices with their start and end apart: 43, of which 16 were waited for; matrix products, arithmetic and copies ran while one was open for 9% of the time, Pallas kernels for 35%

profile of v2, /device:TPU:0, one launch (start us, length us, event | category | flops | bytes accessed | tf_op | source)
XLA Modules:
  0.0 236.4 jit_solution(18137227319922645568)
XLA Ops:
  17.2 12.0 %collective-permute-done.13 = bf16[256,1792]{1,0:T(8,128)(2,1)} collective-permute-done((bf16[256,1792]{1,0:T(8,128)(2,1)}, bf16[256,1792]{1,0:T(8,128)(2,1)}, u32[]{:S(2)}, u32[]{:S(2)}) %collective-permute-start.13) | collective-permute-done | bytes 917536 | tf_op jit(solution)/shard_map/ppermute | solution.py:258
  31.0 7.3 %conditional.12 = (bf16[3,256,1792]{2,1,0:T(8,128)(2,1)}) conditional(s32[]{:T(128)} %bitcast.76, (bf16[256,1792]{1,0:T(8,128)(2,1)}, bf16[256,1792]{1,0:T(8,128)(2,1)}, bf16[256,1792]{1,0:T(8,128)(2,1)}) %tuple.110, (bf16[256,1792]{1,0:T(8,128)(2,1)}, bf16[256,1792]{1,0:T(8,128)(2,1)}, bf16[256,1792]{1,0:T(8,128)(2,1)}) %tuple.110), branch_computations={%region_2.3_spmd, %region_3.4_spmd} | conditional | flops 2752512 | bytes 16515120 | solution.py:286
  39.9 9.0 %collective-permute-done.16 = bf16[256,1792]{1,0:T(8,128)(2,1)} collective-permute-done((bf16[256,1792]{1,0:T(8,128)(2,1)S(1)}, bf16[256,1792]{1,0:T(8,128)(2,1)}, u32[]{:S(2)}, u32[]{:S(2)}) %collective-permute-start.16) | collective-permute-done | bytes 917536 | tf_op jit(solution)/shard_map/ppermute | solution.py:258
  50.7 7.3 %conditional.13 = (bf16[3,256,1792]{2,1,0:T(8,128)(2,1)}) conditional(s32[]{:T(128)} %bitcast.77, (bf16[256,1792]{1,0:T(8,128)(2,1)}, bf16[256,1792]{1,0:T(8,128)(2,1)}, bf16[256,1792]{1,0:T(8,128)(2,1)}) %tuple.113, (bf16[256,1792]{1,0:T(8,128)(2,1)}, bf16[256,1792]{1,0:T(8,128)(2,1)}, bf16[256,1792]{1,0:T(8,128)(2,1)}) %tuple.113), branch_computations={%region_4.5_spmd, %region_5.6_spmd} | conditional | flops 2752512 | bytes 16515120 | solution.py:286
  59.5 8.9 %collective-permute-done.22 = bf16[256,1792]{1,0:T(8,128)(2,1)S(1)} collective-permute-done((bf16[256,1792]{1,0:T(8,128)(2,1)}, bf16[256,1792]{1,0:T(8,128)(2,1)S(1)}, u32[]{:S(2)}, u32[]{:S(2)}) %collective-permute-start.22) | collective-permute-done | bytes 917536 | tf_op jit(solution)/shard_map/ppermute | solution.py:258
  73.0 13.1 %conditional.14 = (bf16[3,256,1792]{2,1,0:T(8,128)(2,1)}, bf16[2,448,28672]{2,1,0:T(8,128)(2,1)}) conditional(s32[]{:T(128)} %bitcast.78, (bf16[256,1792]{1,0:T(8,128)(2,1)S(1)}, bf16[256,1792]{1,0:T(8,128)(2,1)}, bf16[256,1792]{1,0:T(8,128)(2,1)}) %tuple.172, (bf16[256,1792]{1,0:T(8,128)(2,1)S(1)}, bf16[256,1792]{1,0:T(8,128)(2,1)}, ...), branch_computations={%region_6.7_spmd, %region_7.8_spmd} | conditional | flops 6579421184 | bytes 56885264 | solution.py:286
  74.9 11.3 %branch_1_fun.8 = bf16[2,448,28672]{2,1,0:T(8,128)(2,1)} custom-call(s32[2]{0:T(128)S(1)} %get-tuple-element.306.cols_ref, bf16[2,448,1024]{2,1,0:T(8,128)(2,1)S(1)} %get-tuple-element.307.left_ref, bf16[256,1792]{1,0:T(8,128)(2,1)} %get-tuple-element.308.refs_0_, bf16[2,256,1792]{2,1,0:T(8,128)(2,1)} %get-tuple-element.309.refs_1_.refs_5_, ...), custom_call_target="tpu_custom_call" | custom-call | flops 6576668672 | bytes 17432576 | tf_op jit(solution)/shard_map/cond/branch_1_fun/pallas_call | solution.py:134
  89.6 13.4 %conditional.15 = (bf16[3,256,1792]{2,1,0:T(8,128)(2,1)}, bf16[2,448,28672]{2,1,0:T(8,128)(2,1)}) conditional(s32[]{:T(128)} %bitcast.80, (bf16[256,1792]{1,0:T(8,128)(2,1)}, bf16[256,1792]{1,0:T(8,128)(2,1)}, bf16[256,1792]{1,0:T(8,128)(2,1)}, bf16[2,448,28672]{2,1,0:T(8,128)(2,1)}) %tuple.120, (bf16[256,1792]{1,0:T(8,128)(2,1)}, ...), branch_computations={%region_8.9_spmd, %region_9.10_spmd} | conditional | flops 6579421184 | bytes 33947704 | solution.py:286
  91.7 11.3 %branch_1_fun.9 = bf16[2,448,28672]{2,1,0:T(8,128)(2,1)} custom-call(s32[2]{0:T(128)S(1)} %get-tuple-element.322.cols_ref, bf16[2,448,1024]{2,1,0:T(8,128)(2,1)S(1)} %get-tuple-element.323.left_ref, bf16[256,1792]{1,0:T(8,128)(2,1)} %get-tuple-element.324.refs_0_, ...), custom_call_target="tpu_custom_call", output_to_operand_aliasing={{}: (10, {})} | custom-call | flops 6576668672 | bytes 17432576 | tf_op jit(solution)/shard_map/cond/branch_1_fun/pallas_call | solution.py:134
  104.4 7.1 %collective-permute-done.25 = bf16[256,1792]{1,0:T(8,128)(2,1)} collective-permute-done((bf16[256,1792]{1,0:T(8,128)(2,1)}, bf16[256,1792]{1,0:T(8,128)(2,1)}, u32[]{:S(2)}, u32[]{:S(2)}) %collective-permute-start.25) | collective-permute-done | bytes 917536 | tf_op jit(solution)/shard_map/ppermute | solution.py:258
  112.5 9.1 %conditional.16 = (bf16[3,256,1792]{2,1,0:T(8,128)(2,1)}, bf16[2,448,28672]{2,1,0:T(8,128)(2,1)}) conditional(s32[]{:T(128)} %bitcast.81, (bf16[256,1792]{1,0:T(8,128)(2,1)}, bf16[256,1792]{1,0:T(8,128)(2,1)}, bf16[256,1792]{1,0:T(8,128)(2,1)}, bf16[2,448,28672]{2,1,0:T(8,128)(2,1)}) %tuple.124, (bf16[256,1792]{1,0:T(8,128)(2,1)}, ...), branch_computations={%region_10.11_spmd, %region_11.12_spmd} | conditional | flops 3291086848 | bytes 25231416 | solution.py:286
  114.6 7.0 %branch_1_fun.10 = bf16[2,448,28672]{2,1,0:T(8,128)(2,1)} custom-call(s32[1]{0:T(128)} %get-tuple-element.338.cols_ref, bf16[2,448,1024]{2,1,0:T(8,128)(2,1)S(1)} %get-tuple-element.339.left_ref, bf16[256,1792]{1,0:T(8,128)(2,1)} %get-tuple-element.340.refs_0_, bf16[3,256,1792]{2,1,0:T(8,128)(2,1)} %get-tuple-element.341.refs_1_, ...), custom_call_target="tpu_custom_call", output_to_operand_aliasing={{}: (6, {})} | custom-call | flops 3288334336 | bytes 8716288 | tf_op jit(solution)/shard_map/cond/branch_1_fun/pallas_call | solution.py:134
  123.4 7.8 %collective-permute-done.28.refs_0_ = bf16[256,1792]{1,0:T(8,128)(2,1)} collective-permute-done((bf16[256,1792]{1,0:T(8,128)(2,1)}, bf16[256,1792]{1,0:T(8,128)(2,1)}, u32[]{:S(2)}, u32[]{:S(2)}) %collective-permute-start.28) | collective-permute-done | bytes 917536 | tf_op jit(solution)/shard_map/ppermute | solution.py:258
  133.4 8.8 %conditional.17 = (bf16[3,256,1792]{2,1,0:T(8,128)(2,1)}, bf16[2,448,28672]{2,1,0:T(8,128)(2,1)}) conditional(s32[]{:T(128)} %bitcast.82, (bf16[256,1792]{1,0:T(8,128)(2,1)}, bf16[256,1792]{1,0:T(8,128)(2,1)S(1)}, bf16[256,1792]{1,0:T(8,128)(2,1)}, bf16[2,448,28672]{2,1,0:T(8,128)(2,1)}) %tuple.128, (bf16[256,1792]{1,0:T(8,128)(2,1)}, ...), branch_computations={%region_12.13_spmd, %region_13.14_spmd} | conditional | flops 3291086848 | bytes 25231416 | solution.py:286
  135.2 7.0 %branch_1_fun.11 = bf16[2,448,28672]{2,1,0:T(8,128)(2,1)} custom-call(s32[1]{0:T(128)} %get-tuple-element.352.cols_ref, bf16[2,448,1024]{2,1,0:T(8,128)(2,1)S(1)} %get-tuple-element.353.left_ref, bf16[256,1792]{1,0:T(8,128)(2,1)} %get-tuple-element.354.refs_0_, bf16[3,256,1792]{2,1,0:T(8,128)(2,1)} %get-tuple-element.355.refs_1_, ...), custom_call_target="tpu_custom_call", output_to_operand_aliasing={{}: (6, {})} | custom-call | flops 3288334336 | bytes 8716288 | tf_op jit(solution)/shard_map/cond/branch_1_fun/pallas_call | solution.py:134
  143.8 7.0 %collective-permute-done.34 = bf16[256,1792]{1,0:T(8,128)(2,1)} collective-permute-done((bf16[256,1792]{1,0:T(8,128)(2,1)}, bf16[256,1792]{1,0:T(8,128)(2,1)}, u32[]{:S(2)}, u32[]{:S(2)}) %collective-permute-start.34) | collective-permute-done | bytes 917536 | tf_op jit(solution)/shard_map/ppermute | solution.py:258
  153.1 9.1 %conditional.18 = (bf16[3,256,1792]{2,1,0:T(8,128)(2,1)}, bf16[2,448,28672]{2,1,0:T(8,128)(2,1)}) conditional(s32[]{:T(128)} %bitcast.83, (bf16[256,1792]{1,0:T(8,128)(2,1)}, bf16[256,1792]{1,0:T(8,128)(2,1)}, bf16[256,1792]{1,0:T(8,128)(2,1)}, bf16[2,448,28672]{2,1,0:T(8,128)(2,1)}) %tuple.132, (bf16[256,1792]{1,0:T(8,128)(2,1)}, ...), branch_computations={%region_14.15_spmd, %region_15.16_spmd} | conditional | flops 3291086848 | bytes 28901460 | solution.py:286
  172.7 13.4 %conditional.19 = (bf16[3,256,1792]{2,1,0:T(8,128)(2,1)}, bf16[2,448,28672]{2,1,0:T(8,128)(2,1)}) conditional(s32[]{:T(128)} %bitcast.84, (bf16[256,1792]{1,0:T(8,128)(2,1)}, bf16[256,1792]{1,0:T(8,128)(2,1)}, bf16[256,1792]{1,0:T(8,128)(2,1)}, bf16[2,448,28672]{2,1,0:T(8,128)(2,1)}) %tuple.136, (bf16[256,1792]{1,0:T(8,128)(2,1)}, ...), branch_computations={%region_16.17_spmd, %region_17.18_spmd} | conditional | flops 6579421184 | bytes 33947704 | solution.py:286
  174.9 11.3 %branch_1_fun.13 = bf16[2,448,28672]{2,1,0:T(8,128)(2,1)} custom-call(s32[2]{0:T(128)S(1)} %get-tuple-element.380.cols_ref, bf16[2,448,1024]{2,1,0:T(8,128)(2,1)S(1)} %get-tuple-element.381.left_ref, bf16[256,1792]{1,0:T(8,128)(2,1)} %get-tuple-element.382.refs_0_, ...), custom_call_target="tpu_custom_call", output_to_operand_aliasing={{}: (10, {})} | custom-call | flops 6576668672 | bytes 17432576 | tf_op jit(solution)/shard_map/cond/branch_1_fun/pallas_call | solution.py:134
  192.4 13.4 %conditional.20 = (bf16[3,256,1792]{2,1,0:T(8,128)(2,1)}, bf16[2,448,28672]{2,1,0:T(8,128)(2,1)}) conditional(s32[]{:T(128)} %bitcast.85, (bf16[256,1792]{1,0:T(8,128)(2,1)}, bf16[256,1792]{1,0:T(8,128)(2,1)}, bf16[256,1792]{1,0:T(8,128)(2,1)}, bf16[2,448,28672]{2,1,0:T(8,128)(2,1)}) %tuple.140, (bf16[256,1792]{1,0:T(8,128)(2,1)}, ...), branch_computations={%region_18.19_spmd, %region_19.20_spmd} | conditional | flops 6579421184 | bytes 33947704 | solution.py:286
  194.5 11.3 %branch_1_fun.14 = bf16[2,448,28672]{2,1,0:T(8,128)(2,1)} custom-call(s32[2]{0:T(128)S(1)} %get-tuple-element.396.cols_ref, bf16[2,448,1024]{2,1,0:T(8,128)(2,1)S(1)} %get-tuple-element.397.left_ref, bf16[256,1792]{1,0:T(8,128)(2,1)} %get-tuple-element.398.refs_0_, ...), custom_call_target="tpu_custom_call", output_to_operand_aliasing={{}: (10, {})} | custom-call | flops 6576668672 | bytes 17432576 | tf_op jit(solution)/shard_map/cond/branch_1_fun/pallas_call | solution.py:134
  205.8 7.0 %shard_map.18 = bf16[2,448,28672]{2,1,0:T(8,128)(2,1)} custom-call(s32[1]{0:T(128)} %bitcast.71.cols_ref, bf16[2,448,1024]{2,1,0:T(8,128)(2,1)S(1)} %shard_map.17.left_ref, bf16[256,1792]{1,0:T(8,128)(2,1)} %collective-permute-done.28.refs_0_, bf16[3,256,1792]{2,1,0:T(8,128)(2,1)} %get-tuple-element.799.refs_1_, ...), custom_call_target="tpu_custom_call", output_to_operand_aliasing={{}: (6, {})} | custom-call | flops 3288334336 | bytes 8716288 | tf_op jit(solution)/shard_map/pallas_call | solution.py:134
  212.9 8.2 %conditional.21 = (bf16[256,1792]{1,0:T(8,128)(2,1)}, bf16[256,1792]{1,0:T(8,128)(2,1)}, bf16[256,1792]{1,0:T(8,128)(2,1)}, bf16[2,448,28672]{2,1,0:T(8,128)(2,1)}) conditional(s32[]{:T(128)} %bitcast.86, (bf16[256,1792]{1,0:T(8,128)(2,1)}, bf16[256,1792]{1,0:T(8,128)(2,1)}, bf16[256,1792]{1,0:T(8,128)(2,1)}, ...), branch_computations={%region_20.21_spmd, %region_21.22_spmd} | conditional | flops 3288334336 | bytes 19726488 | solution.py:286
  221.0 15.2 %shard_map.19 = bf16[2,448,28672]{2,1,0:T(8,128)(2,1)} custom-call(s32[3]{0:T(128)} %copy-done.4, bf16[2,448,1024]{2,1,0:T(8,128)(2,1)S(1)} %shard_map.17.left_ref, bf16[256,1792]{1,0:T(8,128)(2,1)} %collective-permute-done.35.refs_0_, bf16[3,256,1792]{2,1,0:T(8,128)(2,1)} %get-tuple-element.817.refs_1_, ...), custom_call_target="tpu_custom_call", output_to_operand_aliasing={{}: (14, {})} | custom-call | flops 9865003008 | bytes 26148864 | tf_op jit(solution)/shard_map/pallas_call | solution.py:134
  (114 shorter events, 107.5 us)
Async XLA Ops:
  2.7 26.5 %collective-permute-start.13 = (bf16[256,1792]{1,0:T(8,128)(2,1)}, bf16[256,1792]{1,0:T(8,128)(2,1)}, u32[]{:S(2)}, u32[]{:S(2)}) collective-permute-start(bf16[256,1792]{1,0:T(8,128)(2,1)} %bitcast.89.refs_0_), channel_id=1, source_target_pairs={{0,8},{1,9},{2,10},{3,11},{4,12},{5,13},{6,14},{7,15},{8,16},{9,17... | collective-permute-start | bytes 2752520 | tf_op jit(solution)/shard_map/ppermute | solution.py:258
  5.7 25.3 %collective-permute-start.14 = (bf16[256,1792]{1,0:T(8,128)(2,1)}, bf16[256,1792]{1,0:T(8,128)(2,1)}, u32[]{:S(2)}, u32[]{:S(2)}) collective-permute-start(bf16[256,1792]{1,0:T(8,128)(2,1)} %bitcast.89.refs_0_), channel_id=1, source_target_pairs={{0,4},{1,5},{2,6},{3,7},{4,0},{5,1},{6,2},{7,3},{8,12},{9,13},{10,... | collective-permute-start | bytes 2752520 | tf_op jit(solution)/shard_map/ppermute | solution.py:258
  7.2 23.8 %collective-permute-start.15 = (bf16[256,1792]{1,0:T(8,128)(2,1)}, bf16[256,1792]{1,0:T(8,128)(2,1)}, u32[]{:S(2)}, u32[]{:S(2)}) collective-permute-start(bf16[256,1792]{1,0:T(8,128)(2,1)} %bitcast.89.refs_0_), channel_id=1, source_target_pairs={{0,2},{1,3},{2,0},{3,1},{4,6},{5,7},{6,4},{7,5},{8,10},{9,11},{10,... | collective-permute-start | bytes 2752520 | tf_op jit(solution)/shard_map/ppermute | solution.py:258
  9.0 39.9 %collective-permute-start.16 = (bf16[256,1792]{1,0:T(8,128)(2,1)S(1)}, bf16[256,1792]{1,0:T(8,128)(2,1)}, u32[]{:S(2)}, u32[]{:S(2)}) collective-permute-start(bf16[256,1792]{1,0:T(8,128)(2,1)S(1)} %slice_bitcast_fusion.refs_4_), channel_id=1, source_target_pairs={{0,8},{1,9},{2,10},{3,11},{4,12},{5,13},{6,14},{7,15},{8,16},{9,17... | collective-permute-start | bytes 2752520 | tf_op jit(solution)/shard_map/ppermute | solution.py:258
  15.9 34.7 %collective-permute-start.17 = (bf16[256,1792]{1,0:T(8,128)(2,1)S(1)}, bf16[256,1792]{1,0:T(8,128)(2,1)}, u32[]{:S(2)}, u32[]{:S(2)}) collective-permute-start(bf16[256,1792]{1,0:T(8,128)(2,1)S(1)} %slice_bitcast_fusion.refs_4_), channel_id=1, source_target_pairs={{0,4},{1,5},{2,6},{3,7},{4,0},{5,1},{6,2},{7,3},{8,12},{9,13},{10,... | collective-permute-start | bytes 2752520 | tf_op jit(solution)/shard_map/ppermute | solution.py:258
  38.4 30.1 %collective-permute-start.22 = (bf16[256,1792]{1,0:T(8,128)(2,1)}, bf16[256,1792]{1,0:T(8,128)(2,1)S(1)}, u32[]{:S(2)}, u32[]{:S(2)}) collective-permute-start(bf16[256,1792]{1,0:T(8,128)(2,1)} %collective-permute-done.13), channel_id=1, source_target_pairs={{0,8},{1,9},{2,10},{3,11},{4,12},{5,13},{6,14},{7,15},{8,16},{9,17... | collective-permute-start | bytes 2752520 | tf_op jit(solution)/shard_map/ppermute | solution.py:258
  38.8 34.2 %collective-permute-start.23 = (bf16[256,1792]{1,0:T(8,128)(2,1)}, bf16[256,1792]{1,0:T(8,128)(2,1)}, u32[]{:S(2)}, u32[]{:S(2)}) collective-permute-start(bf16[256,1792]{1,0:T(8,128)(2,1)} %collective-permute-done.15.refs_2_), channel_id=1, source_target_pairs={{0,4},{1,5},{2,6},{3,7},{4,0},{5,1},{6,2},{7,3},{8,12},{9,13},{10,... | collective-permute-start | bytes 2752520 | tf_op jit(solution)/shard_map/ppermute | solution.py:258
  48.9 24.1 %collective-permute-start.24 = (bf16[256,1792]{1,0:T(8,128)(2,1)}, bf16[256,1792]{1,0:T(8,128)(2,1)}, u32[]{:S(2)}, u32[]{:S(2)}) collective-permute-start(bf16[256,1792]{1,0:T(8,128)(2,1)} %collective-permute-done.13), channel_id=1, source_target_pairs={{0,2},{1,3},{2,0},{3,1},{4,6},{5,7},{6,4},{7,5},{8,10},{9,11},{10,... | collective-permute-start | bytes 2752520 | tf_op jit(solution)/shard_map/ppermute | solution.py:258
  58.0 29.7 %collective-permute-start.19 = (bf16[256,1792]{1,0:T(8,128)(2,1)}, bf16[256,1792]{1,0:T(8,128)(2,1)}, u32[]{:S(2)}, u32[]{:S(2)}) collective-permute-start(bf16[256,1792]{1,0:T(8,128)(2,1)} %collective-permute-done.16), channel_id=1, source_target_pairs={{0,8},{1,9},{2,10},{3,11},{4,12},{5,13},{6,14},{7,15},{8,16},{9,17... | collective-permute-start | bytes 2752520 | tf_op jit(solution)/shard_map/ppermute | solution.py:258
  58.2 30.7 %collective-permute-start.20 = (bf16[256,1792]{1,0:T(8,128)(2,1)}, bf16[256,1792]{1,0:T(8,128)(2,1)}, u32[]{:S(2)}, u32[]{:S(2)}) collective-permute-start(bf16[256,1792]{1,0:T(8,128)(2,1)} %collective-permute-done.13), channel_id=1, source_target_pairs={{0,4},{1,5},{2,6},{3,7},{4,0},{5,1},{6,2},{7,3},{8,12},{9,13},{10,... | collective-permute-start | bytes 2752520 | tf_op jit(solution)/shard_map/ppermute | solution.py:258
  86.2 25.3 %collective-permute-start.25 = (bf16[256,1792]{1,0:T(8,128)(2,1)}, bf16[256,1792]{1,0:T(8,128)(2,1)}, u32[]{:S(2)}, u32[]{:S(2)}) collective-permute-start(bf16[256,1792]{1,0:T(8,128)(2,1)} %copy-done), channel_id=1, source_target_pairs={{0,8},{1,9},{2,10},{3,11},{4,12},{5,13},{6,14},{7,15},{8,16},{9,17... | collective-permute-start | bytes 2752520 | tf_op jit(solution)/shard_map/ppermute | solution.py:258
  86.2 26.2 %collective-permute-start.26 = (bf16[256,1792]{1,0:T(8,128)(2,1)}, bf16[256,1792]{1,0:T(8,128)(2,1)}, u32[]{:S(2)}, u32[]{:S(2)}) collective-permute-start(bf16[256,1792]{1,0:T(8,128)(2,1)} %collective-permute-done.16), channel_id=1, source_target_pairs={{0,4},{1,5},{2,6},{3,7},{4,0},{5,1},{6,2},{7,3},{8,12},{9,13},{10,... | collective-permute-start | bytes 2752520 | tf_op jit(solution)/shard_map/ppermute | solution.py:258
  87.8 24.6 %collective-permute-start.27 = (bf16[256,1792]{1,0:T(8,128)(2,1)}, bf16[256,1792]{1,0:T(8,128)(2,1)}, u32[]{:S(2)}, u32[]{:S(2)}) collective-permute-start(bf16[256,1792]{1,0:T(8,128)(2,1)} %collective-permute-done.16), channel_id=1, source_target_pairs={{0,2},{1,3},{2,0},{3,1},{4,6},{5,7},{6,4},{7,5},{8,10},{9,11},{10,... | collective-permute-start | bytes 2752520 | tf_op jit(solution)/shard_map/ppermute | solution.py:258
  103.0 28.1 %collective-permute-start.28 = (bf16[256,1792]{1,0:T(8,128)(2,1)}, bf16[256,1792]{1,0:T(8,128)(2,1)}, u32[]{:S(2)}, u32[]{:S(2)}) collective-permute-start(bf16[256,1792]{1,0:T(8,128)(2,1)} %collective-permute-done.19), channel_id=1, source_target_pairs={{0,8},{1,9},{2,10},{3,11},{4,12},{5,13},{6,14},{7,15},{8,16},{9,17... | collective-permute-start | bytes 2752520 | tf_op jit(solution)/shard_map/ppermute | solution.py:258
  103.5 28.5 %collective-permute-start.29 = (bf16[256,1792]{1,0:T(8,128)(2,1)}, bf16[256,1792]{1,0:T(8,128)(2,1)S(1)}, u32[]{:S(2)}, u32[]{:S(2)}) collective-permute-start(bf16[256,1792]{1,0:T(8,128)(2,1)} %copy-done), channel_id=1, source_target_pairs={{0,4},{1,5},{2,6},{3,7},{4,0},{5,1},{6,2},{7,3},{8,12},{9,13},{10,... | collective-permute-start | bytes 2752520 | tf_op jit(solution)/shard_map/ppermute | solution.py:258
  121.6 29.2 %collective-permute-start.34 = (bf16[256,1792]{1,0:T(8,128)(2,1)}, bf16[256,1792]{1,0:T(8,128)(2,1)}, u32[]{:S(2)}, u32[]{:S(2)}) collective-permute-start(bf16[256,1792]{1,0:T(8,128)(2,1)} %collective-permute-done.23), channel_id=1, source_target_pairs={{0,8},{1,9},{2,10},{3,11},{4,12},{5,13},{6,14},{7,15},{8,16},{9,17... | collective-permute-start | bytes 2752520 | tf_op jit(solution)/shard_map/ppermute | solution.py:258
  121.8 29.9 %collective-permute-start.35 = (bf16[256,1792]{1,0:T(8,128)(2,1)}, bf16[256,1792]{1,0:T(8,128)(2,1)}, u32[]{:S(2)}, u32[]{:S(2)}) collective-permute-start(bf16[256,1792]{1,0:T(8,128)(2,1)} %collective-permute-done.19), channel_id=1, source_target_pairs={{0,4},{1,5},{2,6},{3,7},{4,0},{5,1},{6,2},{7,3},{8,12},{9,13},{10,... | collective-permute-start | bytes 2752520 | tf_op jit(solution)/shard_map/ppermute | solution.py:258
  142.2 28.2 %collective-permute-start.31 = (bf16[256,1792]{1,0:T(8,128)(2,1)}, bf16[256,1792]{1,0:T(8,128)(2,1)}, u32[]{:S(2)}, u32[]{:S(2)}) collective-permute-start(bf16[256,1792]{1,0:T(8,128)(2,1)} %collective-permute-done.21), channel_id=1, source_target_pairs={{0,8},{1,9},{2,10},{3,11},{4,12},{5,13},{6,14},{7,15},{8,16},{9,17... | collective-permute-start | bytes 2752520 | tf_op jit(solution)/shard_map/ppermute | solution.py:258
  142.3 29.1 %collective-permute-start.32 = (bf16[256,1792]{1,0:T(8,128)(2,1)}, bf16[256,1792]{1,0:T(8,128)(2,1)}, u32[]{:S(2)}, u32[]{:S(2)}) collective-permute-start(bf16[256,1792]{1,0:T(8,128)(2,1)} %collective-permute-done.28.refs_0_), channel_id=1, source_target_pairs={{0,4},{1,5},{2,6},{3,7},{4,0},{5,1},{6,2},{7,3},{8,12},{9,13},{10,... | collective-permute-start | bytes 2752520 | tf_op jit(solution)/shard_map/ppermute | solution.py:258
  162.2 27.5 %collective-permute-start.40 = (bf16[256,1792]{1,0:T(8,128)(2,1)}, bf16[256,1792]{1,0:T(8,128)(2,1)}, u32[]{:S(2)}, u32[]{:S(2)}) collective-permute-start(bf16[256,1792]{1,0:T(8,128)(2,1)} %collective-permute-done.34), channel_id=1, source_target_pairs={{0,8},{1,9},{2,10},{3,11},{4,12},{5,13},{6,14},{7,15},{8,16},{9,17... | collective-permute-start | bytes 2752520 | tf_op jit(solution)/shard_map/ppermute | solution.py:258
  162.3 28.4 %collective-permute-start.41 = (bf16[256,1792]{1,0:T(8,128)(2,1)}, bf16[256,1792]{1,0:T(8,128)(2,1)}, u32[]{:S(2)}, u32[]{:S(2)}) collective-permute-start(bf16[256,1792]{1,0:T(8,128)(2,1)} %collective-permute-done.25), channel_id=1, source_target_pairs={{0,4},{1,5},{2,6},{3,7},{4,0},{5,1},{6,2},{7,3},{8,12},{9,13},{10,... | collective-permute-start | bytes 2752520 | tf_op jit(solution)/shard_map/ppermute | solution.py:258
  186.2 26.6 %collective-permute-start.37 = (bf16[256,1792]{1,0:T(8,128)(2,1)}, bf16[256,1792]{1,0:T(8,128)(2,1)}, u32[]{:S(2)}, u32[]{:S(2)}) collective-permute-start(bf16[256,1792]{1,0:T(8,128)(2,1)} %collective-permute-done.31), channel_id=1, source_target_pairs={{0,8},{1,9},{2,10},{3,11},{4,12},{5,13},{6,14},{7,15},{8,16},{9,17... | collective-permute-start | bytes 2752520 | tf_op jit(solution)/shard_map/ppermute | solution.py:258
  186.2 26.6 %collective-permute-start.38 = (bf16[256,1792]{1,0:T(8,128)(2,1)}, bf16[256,1792]{1,0:T(8,128)(2,1)}, u32[]{:S(2)}, u32[]{:S(2)}) collective-permute-start(bf16[256,1792]{1,0:T(8,128)(2,1)} %collective-permute-done.33), channel_id=1, source_target_pairs={{0,4},{1,5},{2,6},{3,7},{4,0},{5,1},{6,2},{7,3},{8,12},{9,13},{10,... | collective-permute-start | bytes 2752520 | tf_op jit(solution)/shard_map/ppermute | solution.py:258
  189.7 23.1 %collective-permute-start.39 = (bf16[256,1792]{1,0:T(8,128)(2,1)}, bf16[256,1792]{1,0:T(8,128)(2,1)}, u32[]{:S(2)}, u32[]{:S(2)}) collective-permute-start(bf16[256,1792]{1,0:T(8,128)(2,1)} %collective-permute-done.32.refs_8_), channel_id=1, source_target_pairs={{0,2},{1,3},{2,0},{3,1},{4,6},{5,7},{6,4},{7,5},{8,10},{9,11},{10,... | collective-permute-start | bytes 2752520 | tf_op jit(solution)/shard_map/ppermute | solution.py:258
  (26 other events, 484.9 us)
